TPU v7x, 128 devices: a whole 4x4x4 slice. The times are simulated.
128 devices in a mesh: dp: 8 (over z, core), ctx: 16 (over x, y).
Axes of the slice: x: 4, y: 4, z: 4, core: 2. Of those that a mesh axis runs over, the one named last changes fastest.
Arguments:
- queries: bfloat16 [8, 2048, 64, 576], P('dp', 'ctx'), may hold values from -29.108076 to 29.108076
- latents: bfloat16 [8, 2048, 576], P('dp', 'ctx'), may hold values from -4.5 to 4.5
- out_grad: bfloat16 [8, 2048, 64, 512], P('dp', 'ctx'), may hold values from -6 to 6
- layer_input: bfloat16 [8, 2048, 5120], P('dp', 'ctx'), may hold values from -0.125 to 0.125
- block_list: int32 [8, 16, 4], P('dp'), may hold values from -1 to 15, as said below
Outputs:
- latent_grad: float32 [8, 2048, 576], P('dp', 'ctx')
- weight_grad: float32 [5120, 576], P('ctx')
Inputs may be any that keep to these rules, and one draw needn't show every extreme that they name: `block_list`: row (s, b) lists block b, then the 1 block before it (-1 where they would fall before block 0), then up to 2 distinct blocks drawn among those before the window (-1 in the slots left empty). No row names a block twice.
All inputs are finite; a program needn't handle non-finite values.
Results may differ from a plain program's by a relative error of at most 0.035.
Values may be sent and summed in bfloat16 or wider, within the bound.
A program may use at most 128 MiB of HBM per device.

v0:
```python
import math

import jax
import jax.numpy as jnp
from jax import lax
from jax.sharding import PartitionSpec as P

R = 512
ROPE = 64
NOPE = 128
SLOTS = 4


def make_visible(row_list, query_block, heads_row, block_len):
    token_row = jnp.arange(block_len * heads_row, dtype=jnp.int32) // heads_row
    position = jnp.arange(SLOTS * block_len, dtype=jnp.int32)
    entry = row_list[position // block_len]
    inner = position % block_len
    listed = (entry >= 0)[None, :]
    earlier = (entry != query_block)[None, :] | (inner[None, :] <= token_row[:, None])
    return listed & earlier


def block_grads(query_rows, grad_rows, keys_flat, visible, scale):
    scores = jnp.dot(query_rows, keys_flat.T, preferred_element_type=jnp.float32) * scale
    scores = jnp.where(visible, scores, -jnp.inf)
    top = jnp.max(scores, axis=1, keepdims=True)
    weights = jnp.exp(scores - top)
    probs = weights / jnp.sum(weights, axis=1, keepdims=True)
    probs_b = probs.astype(jnp.bfloat16)
    values = keys_flat[:, :R]
    output = jnp.dot(probs_b, values, preferred_element_type=jnp.float32)
    delta = jnp.sum(grad_rows.astype(jnp.float32) * output, axis=1, keepdims=True)
    dprob = jnp.dot(grad_rows, values.T, preferred_element_type=jnp.float32)
    dscore = (probs * (dprob - delta) * scale).astype(jnp.bfloat16)
    key_grad = jnp.dot(dscore.T, query_rows, preferred_element_type=jnp.float32)
    value_grad = jnp.dot(probs_b.T, grad_rows, preferred_element_type=jnp.float32)
    return jnp.concatenate([key_grad[:, :R] + value_grad, key_grad[:, R:]], axis=1)


def attend(own_queries, own_grad, keys_cat, row_list, own_block):
    block_len, heads, width = own_queries.shape
    scale = (NOPE + ROPE) ** (-0.5)
    group = math.gcd(heads, max(1, 2048 // block_len))
    keys_flat = keys_cat.reshape(SLOTS * block_len, width)
    visible = make_visible(row_list, own_block, group, block_len)

    def group_step(index, total):
        query_rows = lax.dynamic_slice_in_dim(own_queries, index * group, group, 1).reshape(
            block_len * group, width
        )
        grad_rows = lax.dynamic_slice_in_dim(own_grad, index * group, group, 1).reshape(
            block_len * group, R
        )
        parts = block_grads(query_rows, grad_rows, keys_flat, visible, scale)
        return total + parts.reshape(SLOTS, block_len, width)

    start_total = jnp.zeros((SLOTS, block_len, width), jnp.float32)
    return lax.fori_loop(0, heads // group, group_step, start_total)


def token_inner(left, right):
    return lax.dot_general(
        left, right, (((0,), (0,)), ((), ())), preferred_element_type=jnp.float32
    )


def per_device(queries, latents, out_grad, layer_input, block_list):
    own_queries = queries[0]
    own_grad = out_grad[0]
    own_latents = latents[0]
    block_len, width = own_latents.shape
    blocks = lax.axis_size("ctx")
    own_block = lax.axis_index("ctx")
    row_list = lax.dynamic_index_in_dim(block_list[0], own_block, 0, keepdims=False)
    every = lax.all_gather(own_latents, "ctx", axis=0, tiled=True).reshape(blocks, block_len, width)
    keys_cat = every[jnp.maximum(row_list, 0)]
    parts = attend(own_queries, own_grad, keys_cat, row_list, own_block)
    one_hot = (jnp.arange(blocks, dtype=jnp.int32)[:, None] == row_list[None, :]).astype(
        jnp.float32
    )
    spread = jnp.einsum("be,etk->btk", one_hot, parts, precision=lax.Precision.HIGHEST)
    latent_grad = lax.psum_scatter(
        spread.reshape(blocks * block_len, width), "ctx", scatter_dimension=0, tiled=True
    )
    grad_b = latent_grad.astype(jnp.bfloat16)
    own_input = layer_input[0]
    columns = own_input.shape[1] // blocks
    summed = lax.psum(token_inner(own_input, grad_b), ("dp", "ctx"))
    weight_grad = lax.dynamic_slice_in_dim(summed, own_block * columns, columns, 0)
    return (latent_grad[None], weight_grad)


def solution(mesh):
    placed = (
        P("dp", "ctx", None, None),
        P("dp", "ctx", None),
        P("dp", "ctx", None, None),
        P("dp", "ctx", None),
        P("dp", None, None),
    )
    return jax.shard_map(
        per_device,
        mesh=mesh,
        in_specs=placed,
        out_specs=(P("dp", "ctx", None), P("ctx", None)),
        check_vma=False,
    )
```

profile of v0, /device:TPU:1, one launch (start us, length us, event | category | flops | bytes accessed | tf_op | source)
XLA Modules:
  0.0 451.6 jit_solution(13079860395261132539)
XLA Ops:
  8.0 14.8 %copy.20 = bf16[1,128,64,576]{3,2,1,0:T(8,128)(2,1)} copy(bf16[1,128,64,576]{1,3,2,0:T(8,128)(2,1)} %param.7) | data formatting | bytes 18874368 | tf_op args[0]
  24.1 2.7 compare_reduce_fusion
  26.8 34.4 %all-gather.3.cloned.1.call-done = bf16[1,2048,576]{1,2,0:T(8,128)(2,1)} async-done(((bf16[1,128,576]{1,2,0:T(8,128)(2,1)}), bf16[1,2048,576]{1,2,0:T(8,128)(2,1)}) %all-gather.3.cloned.1.call-update) | async-done | bytes 2359312 | tf_op jit(solution)/shard_map/all_gather | solution.py:76
  61.2 2.4 copy.28
  65.6 2.3 gather_fusion
  69.0 113.0 %while.14 = (s32[]{:T(128)}, f32[4,128,576]{1,0,2:T(4,128)}, bf16[128,64,576]{2,1,0:T(8,128)(2,1)}, bf16[512,576]{1,0:T(8,128)(2,1)}, bf16[128,64,512]{2,1,0:T(8...) while((s32[]{:T(128)}, f32[4,128,576]{1,0,2:T(4,128)}, ...), condition=%wide.region_4.5_spmd.clone, body=%wide.region_0.4_spmd.clone.sunk | while | flops 5662402560 | bytes 95980880 | solution.py:59
  70.8 2.5 copy.33
  73.3 2.0 constant_dynamic-slice_fusion.7
  82.1 6.9 %fusion.56 = f32[512,576]{0,1:T(8,128)} fusion(bf16[2048,576]{1,0:T(8,128)(2,1)} %bitcast.55, bf16[2048,512]{1,0:T(8,128)(2,1)S(1)} %bitcast.52, f32[2048]{0:T(1024)S(1)} %multiply_reduce_fusion.2, f32[2048]{0:T(1024)S(1)} %fusion.55, f32[2048,512]{0,1:T(8,128)} %copy-done.1, f32[2048]{0:T(1024)S(1)} %get-tuple-element.261, ...), kind=kOutput, calls=%fused_computation.10.clone.1 | convolution fusion | flops 2287992832 | bytes 10641408 | tf_op jit(solution)/shard_map/while/body/eval_jaxpr/dot_general | solution.py:36
  89.0 3.8 convolution_add_fusion.2
  94.3 2.7 select_add_fusion.2
  98.8 2.5 copy.33
  101.3 2.0 constant_dynamic-slice_fusion.7
  103.4 2.0 fusion.54
  110.1 6.8 %fusion.56 = f32[512,576]{0,1:T(8,128)} fusion(bf16[2048,576]{1,0:T(8,128)(2,1)} %bitcast.55, bf16[2048,512]{1,0:T(8,128)(2,1)S(1)} %bitcast.52, f32[2048]{0:T(1024)S(1)} %multiply_reduce_fusion.2, f32[2048]{0:T(1024)S(1)} %fusion.55, f32[2048,512]{0,1:T(8,128)} %copy-done.1, f32[2048]{0:T(1024)S(1)} %get-tuple-element.261, ...), kind=kOutput, calls=%fused_computation.10.clone.1 | convolution fusion | flops 2287992832 | bytes 10641408 | tf_op jit(solution)/shard_map/while/body/eval_jaxpr/dot_general | solution.py:36
  117.0 3.8 convolution_add_fusion.2
  122.3 3.0 select_add_fusion.2
  127.1 2.5 copy.33
  129.6 2.0 constant_dynamic-slice_fusion.7
  138.4 6.8 %fusion.56 = f32[512,576]{0,1:T(8,128)} fusion(bf16[2048,576]{1,0:T(8,128)(2,1)} %bitcast.55, bf16[2048,512]{1,0:T(8,128)(2,1)S(1)} %bitcast.52, f32[2048]{0:T(1024)S(1)} %multiply_reduce_fusion.2, f32[2048]{0:T(1024)S(1)} %fusion.55, f32[2048,512]{0,1:T(8,128)} %copy-done.1, f32[2048]{0:T(1024)S(1)} %get-tuple-element.261, ...), kind=kOutput, calls=%fused_computation.10.clone.1 | convolution fusion | flops 2287992832 | bytes 10641408 | tf_op jit(solution)/shard_map/while/body/eval_jaxpr/dot_general | solution.py:36
  145.3 3.8 convolution_add_fusion.2
  150.6 3.0 select_add_fusion.2
  155.5 2.5 copy.33
  157.9 2.0 constant_dynamic-slice_fusion.7
  166.8 6.8 %fusion.56 = f32[512,576]{0,1:T(8,128)} fusion(bf16[2048,576]{1,0:T(8,128)(2,1)} %bitcast.55, bf16[2048,512]{1,0:T(8,128)(2,1)S(1)} %bitcast.52, f32[2048]{0:T(1024)S(1)} %multiply_reduce_fusion.2, f32[2048]{0:T(1024)S(1)} %fusion.55, f32[2048,512]{0,1:T(8,128)} %copy-done.1, f32[2048]{0:T(1024)S(1)} %get-tuple-element.261, ...), kind=kOutput, calls=%fused_computation.10.clone.1 | convolution fusion | flops 2287992832 | bytes 10641408 | tf_op jit(solution)/shard_map/while/body/eval_jaxpr/dot_general | solution.py:36
  173.6 3.8 convolution_add_fusion.2
  179.0 3.0 select_add_fusion.2
  182.0 3.5 fusion.21
  185.6 4.3 copy.31
  190.0 77.1 %reduce-scatter.2.cloned.1.call-done = f32[128,576]{0,1:T(8,128)} async-done(((f32[2048,576]{0,1:T(8,128)}), f32[128,576]{0,1:T(8,128)}) %reduce-scatter.2.cloned.1.call-update) | async-done | bytes 294928 | tf_op jit(solution)/shard_map/reduce_scatter | solution.py:83
  267.0 6.9 %convolution_bitcast_fusion = f32[5120,576]{0,1:T(8,128)} fusion(bf16[1,128,5120]{2,1,0:T(8,128)(2,1)S(1)} %copy-done, f32[128,576]{0,1:T(8,128)} %reduce-scatter.2.cloned.1.call-done), kind=kOutput, calls=%fused_computation.18 | convolution fusion | flops 755048448 | bytes 13402112 | tf_op jit(solution)/shard_map/dot_general | solution.py:63
  274.0 168.3 %all-reduce.2.cloned.1.call-done = f32[5120,576]{0,1:T(8,128)} async-done(((f32[5120,576]{0,1:T(8,128)}), f32[5120,576]{0,1:T(8,128)}) %all-reduce.2.cloned.1.call-update) | async-done | bytes 11796496 | tf_op jit(solution)/shard_map/psum | solution.py:89
  (85 shorter events, 46.0 us)
Async XLA Ops:
  7.2 259.9 %copy-start = (bf16[1,128,5120]{2,1,0:T(8,128)(2,1)S(1)}, bf16[1,128,5120]{2,1,0:T(8,128)(2,1)}, u32[]{:S(2)}) copy-start(bf16[1,128,5120]{2,1,0:T(8,128)(2,1)} %param.10) | copy-start | bytes 3932164
  7.2 54.0 %all-gather.3.cloned.1.call-start = ((), (), s32[]{:S(2)}) async-start(), calls=%async_computation.3 | async-start | bytes 2506752 | tf_op jit(solution)/shard_map/all_gather | solution.py:76
  7.9 259.1 %reduce-scatter.2.cloned.1.call-start = ((), (), s32[]{:S(2)}) async-start(), calls=%async_computation.1 | async-start | bytes 5013504 | tf_op jit(solution)/shard_map/reduce_scatter | solution.py:83
  8.0 14.8 %copy-start.6 = (s32[1,16,4]{1,2,0:T(4,128)S(1)}, s32[1,16,4]{1,2,0:T(4,128)}, u32[]{:S(2)}) copy-start(s32[1,16,4]{1,2,0:T(4,128)} %param.11) | copy-start | bytes 772
  69.0 113.0 %copy-start.5 = (s32[4]{0:T(128)S(1)}, s32[4]{0:T(128)}, u32[]{:S(2)}) copy-start(s32[4]{0:T(128)} %get-tuple-element.174) | copy-start | bytes 52
  73.3 2.1 copy-start.4
  75.4 2.1 copy-start.2
  77.4 2.1 copy-start.1
  77.4 3.1 copy-start.3
  89.0 3.8 slice-start
  101.3 2.1 copy-start.4
  103.3 2.1 copy-start.2
  105.4 2.1 copy-start.1
  105.4 3.1 copy-start.3
  117.0 3.8 slice-start
  129.6 2.1 copy-start.4
  131.7 2.1 copy-start.2
  133.7 2.1 copy-start.1
  133.8 3.1 copy-start.3
  145.3 3.8 slice-start
  157.9 2.1 copy-start.4
  160.0 2.1 copy-start.2
  162.1 2.1 copy-start.1
  162.1 3.1 copy-start.3
  173.6 3.8 slice-start
  189.9 252.3 %all-reduce.2.cloned.1.call-start = ((), (), s32[]{:S(2)}) async-start(), calls=%async_computation.2 | async-start | bytes 23592960 | tf_op jit(solution)/shard_map/psum | solution.py:89
Sparse Core Ops, SparseCore 0:
  10.1 51.0 all-gather.2
  190.0 76.9 reduce-scatter.1
  274.1 168.1 all-reduce.1
where the time goes:
time: 453 us; the launch traced here: 452 us
  waiting for transfers between devices  280 us (62%)
  local copies, waits for them, and re-layouts  71.1 us (16%)
  matrix products  67.6 us (15%)
  other arithmetic  18.1 us (4%)
  between operations  13.8 us (3%)
    psum x1, waiting for transfers between devices, per_device(): summed = lax.psum(token_inner(own_input, grad_b), ('dp', 'ctx'))  168 us
    reduce_scatter x1, waiting for transfers between devices, per_device(): lax.psum_scatter(spread.reshape(blocks * block_len, width), 'ctx', scatte...  77.1 us
    all_gather x1, waiting for transfers between devices, per_device(): lax.all_gather(own_latents, 'ctx', axis=0, tiled=True)  34.4 us
    dot_general x4, matrix products, block_grads(): key_grad = jnp.dot(dscore.T, query_rows, preferred_element_type=jnp.float32)  27.4 us
    unnamed x11, local copies, waits for them, and re-layouts  23.8 us
    dot_general x4, matrix products, block_grads(): jnp.dot(probs_b.T, grad_rows, preferred_element_type=jnp.float32)  15.3 us
    add x4, other arithmetic, group_step(): return total + parts.reshape(SLOTS, block_len, width)  11.8 us
    reshape x4, local copies, waits for them, and re-layouts, group_step(): lax.dynamic_slice_in_dim(own_grad, index * group, group, 1)  9.92 us
  transfers between devices with their start and end apart: 3, of which 3 were waited for; matrix products, arithmetic and copies ran while one was open for 4% of the time, Pallas kernels for 0%

commit v1 on v0

v1 whole, which is shorter than its diff:
```python
import functools

import jax
import jax.numpy as jnp
from jax import lax
from jax.experimental import pallas as pl
from jax.experimental.pallas import tpu as pltpu
from jax.sharding import PartitionSpec as P

R = 512
W = 576
HALF = 288
TOK = 128
SLOTS = 4
SIDE = 4
SCALE = 192 ** -0.5
LOG2E = 1.4426950408889634
NT = (((1,), (1,)), ((), ()))
MESH = pl.DeviceIdType.MESH
F32 = jnp.float32
BF16 = jnp.bfloat16


def place():
    me = lax.axis_index("ctx")
    return me, me // SIDE, me % SIDE


def ctx_at(x, y):
    return (x % SIDE) * SIDE + y % SIDE


def remote(src, dst, send, recv, device):
    return pltpu.make_async_remote_copy(
        src_ref=src, dst_ref=dst, send_sem=send, recv_sem=recv, device_id=device, device_id_type=MESH
    )


def greet(devices):
    barrier = pltpu.get_barrier_semaphore()
    for device in devices:
        pl.semaphore_signal(barrier, inc=1, device_id=device, device_id_type=MESH)
    pl.semaphore_wait(barrier, len(devices))


def line_peers(x, y):
    return [{"ctx": ctx_at(x + d, y)} for d in (1, 2, 3)] + [{"ctx": ctx_at(x, y + d)} for d in (1, 2, 3)]


def plane_gather(every, x, y, send, recv):
    top, low = pl.ds(0, HALF), pl.ds(HALF, HALF)

    def copy(bx, by, rows, k, dx, dy):
        piece = every.at[ctx_at(bx, by), rows]
        return remote(piece, piece, send.at[k], recv.at[k], {"ctx": ctx_at(x + dx, y + dy)})

    started = []

    def start(*args):
        c = copy(*args)
        c.start()
        started.append(c)

    for d in (1, 3, 2):
        start(x, y, top, d - 1, d, 0)
        start(x, y, low, 3 + d - 1, 0, d)
    for j in (0, 1, 3, 2):
        if j > 0:
            copy(x - j, y, top, j - 1, j, 0).wait_recv()
            copy(x, y - j, low, 3 + j - 1, 0, j).wait_recv()
        for d in (1, 3, 2):
            start(x - j, y, top, 6 + 3 * j + d - 1, 0, d)
            start(x, y - j, low, 18 + 3 * j + d - 1, d, 0)
    for j in (0, 1, 3, 2):
        for d in (1, 3, 2):
            copy(x - j, y - d, top, 6 + 3 * j + d - 1, 0, d).wait_recv()
            copy(x - d, y - j, low, 18 + 3 * j + d - 1, d, 0).wait_recv()
    for c in started:
        c.wait_send()


def gather_kernel(lat_ref, every_ref, send, recv, own_sem):
    me, x, y = place()
    own = pltpu.make_async_copy(lat_ref.at[0], every_ref.at[me], own_sem)
    own.start()
    greet(line_peers(x, y))
    own.wait()
    plane_gather(every_ref, x, y, send, recv)


def gather_latents(latents):
    return pl.pallas_call(
        gather_kernel,
        out_shape=jax.ShapeDtypeStruct((16, W, TOK), BF16),
        in_specs=[pl.BlockSpec(memory_space=pl.ANY)],
        out_specs=pl.BlockSpec(memory_space=pl.ANY),
        scratch_shapes=[pltpu.SemaphoreType.DMA((30,)), pltpu.SemaphoreType.DMA((30,)), pltpu.SemaphoreType.DMA],
        compiler_params=pltpu.CompilerParams(collective_id=0, has_side_effects=True),
        name="gather_latents",
    )(latents)


def attn_kernel(heads, sub, lst, k0, k1, k2, k3, qt_ref, do_ref, own_ref, parts_ref, acc, k_scr, d_scr):
    step = pl.program_id(0)

    @pl.when(step == 0)
    def _():
        for e, k_ref in enumerate((k0, k1, k2, k3)):
            k_scr[e * TOK : (e + 1) * TOK, :] = k_ref[0].T
        acc[...] = jnp.zeros_like(acc)

    tg = 256 // heads
    ri = lax.broadcasted_iota(jnp.int32, (256, 256), 0)
    ci = lax.broadcasted_iota(jnp.int32, (256, 256), 1)
    perm = jnp.where((ri // tg == ci % heads) & (ri % tg == ci // heads), 1.0, 0.0).astype(BF16)
    for g in range(TOK // tg):
        rows = do_ref[g * tg : (g + 1) * tg].reshape(256, R)
        moved = jnp.dot(perm, rows, preferred_element_type=F32)
        d_scr[:, g * tg : (g + 1) * tg, :] = moved.astype(BF16).reshape(heads, tg, R)
    key_at = lax.broadcasted_iota(jnp.int32, (TOK, TOK), 0)
    tok_at = lax.broadcasted_iota(jnp.int32, (TOK, TOK), 1)
    causal = jnp.concatenate([key_at <= tok_at] * sub, axis=1)
    away = [None] + [jnp.where(lst[e] >= 0, 0.0, jnp.inf) for e in range(1, SLOTS)]
    c = SCALE * LOG2E
    keys = k_scr[...]
    for j in range(heads // sub):
        qt = jnp.concatenate([qt_ref[j * sub + i] for i in range(sub)], axis=1)
        d = d_scr[j * sub : (j + 1) * sub].reshape(sub * TOK, R)
        s = jnp.dot(keys, qt, preferred_element_type=F32)
        dp = lax.dot_general(keys[:, :R], d, NT, preferred_element_type=F32)
        ss = [s[e * TOK : (e + 1) * TOK] for e in range(SLOTS)]
        ss[0] = jnp.where(causal, ss[0], -jnp.inf)
        top = jnp.max(ss[0], axis=0, keepdims=True)
        for e in range(1, SLOTS):
            top = jnp.maximum(top, jnp.max(ss[e], axis=0, keepdims=True) - away[e])
        mc = top * c
        p = jnp.concatenate(
            [jnp.exp2(ss[e] * c - (mc if e == 0 else mc + away[e])) for e in range(SLOTS)], axis=0
        )
        inv = 1.0 / jnp.sum(p, axis=0, keepdims=True)
        delta = jnp.sum(p * dp, axis=0, keepdims=True) * inv
        probs = p * inv
        ds = (probs * (dp - delta)).astype(BF16)
        pb = probs.astype(BF16)
        kg = lax.dot_general(ds, qt, NT, preferred_element_type=F32) * SCALE
        vg = jnp.dot(pb, d, preferred_element_type=F32)
        acc[:, :R] += kg[:, :R] + vg
        acc[:, R:] += kg[:, R:]

    @pl.when(step == pl.num_programs(0) - 1)
    def _():
        own_ref[...] = acc[:TOK].T
        for e in range(1, SLOTS):
            parts_ref[e - 1] = acc[e * TOK : (e + 1) * TOK].T.astype(BF16)


def attention(row, every, qt, do, heads=16, sub=4):
    n_heads = qt.shape[0]
    spec = lambda e: pl.BlockSpec((1, W, TOK), lambda g, l: (jnp.maximum(l[e], 0), 0, 0))
    return pl.pallas_call(
        functools.partial(attn_kernel, heads, sub),
        grid_spec=pltpu.PrefetchScalarGridSpec(
            num_scalar_prefetch=1,
            grid=(n_heads // heads,),
            in_specs=[spec(e) for e in range(SLOTS)]
            + [
                pl.BlockSpec((heads, W, TOK), lambda g, l: (g, 0, 0)),
                pl.BlockSpec((TOK, heads, R), lambda g, l: (0, g, 0)),
            ],
            out_specs=[
                pl.BlockSpec((W, TOK), lambda g, l: (0, 0)),
                pl.BlockSpec((SLOTS - 1, W, TOK), lambda g, l: (0, 0, 0)),
            ],
            scratch_shapes=[
                pltpu.VMEM((SLOTS * TOK, W), F32),
                pltpu.VMEM((SLOTS * TOK, W), BF16),
                pltpu.VMEM((heads, TOK, R), BF16),
            ],
        ),
        out_shape=[
            jax.ShapeDtypeStruct((W, TOK), F32),
            jax.ShapeDtypeStruct((SLOTS - 1, W, TOK), BF16),
        ],
        compiler_params=pltpu.CompilerParams(vmem_limit_bytes=56 * 2**20),
        cost_estimate=pl.CostEstimate(flops=22 * 10**9, bytes_accessed=20 * 10**6, transcendentals=4 * 10**6),
        name="attention",
    )(row, every, every, every, every, qt, do)


def tail_kernel(
    lst, own_ref, parts_ref, xt_ref, lat_ref, w_ref,
    raw, mid, back, near, every, pieces, arrived, total, totals,
    raw_s, raw_r, mid_s, mid_r, near_s, near_r, all_s, all_r, dp_s, dp_r, sum_s, sum_r,
):
    me, x, y = place()
    dp = lax.axis_index("dp")
    n_dp = pieces.shape[0]
    greet(
        line_peers(x, y)
        + [{"ctx": (me + 1) % 16}, {"ctx": (me + 15) % 16}]
        + [{"dp": (dp + d) % n_dp} for d in range(1, n_dp)]
    )
    halves = (pl.ds(0, HALF), pl.ds(HALF, HALF))
    started = []

    def start(c):
        c.start()
        started.append(c)

    def raw_copy(half, d):
        return remote(
            parts_ref.at[pl.ds(1, 2), halves[half]],
            raw.at[half, d - 1],
            raw_s.at[half, d - 1],
            raw_r.at[half, d - 1],
            {"ctx": ctx_at(x, y + d) if half == 0 else ctx_at(x + d, y)},
        )

    for d in (1, 3, 2):
        for half in (0, 1):
            start(raw_copy(half, d))
    near_copy = remote(parts_ref.at[0], near, near_s, near_r, {"ctx": (me + 15) % 16})
    start(near_copy)

    def mid_copy(half, d):
        return remote(
            mid.at[half, d - 1],
            back.at[half, d - 1],
            mid_s.at[half, d - 1],
            mid_r.at[half, d - 1],
            {"ctx": ctx_at(x + d, y) if half == 0 else ctx_at(x, y + d)},
        )

    kept = []
    for half in (0, 1):
        found = []
        for d in range(SIDE):
            src = ctx_at(x, y - d) if half == 0 else ctx_at(x - d, y)
            if d > 0:
                raw_copy(half, d).wait_recv()
            for e in range(2):
                part = parts_ref[1 + e, halves[half]] if d == 0 else raw[half, d - 1, e]
                found.append((lst[src, 2 + e], part.astype(F32)))
        for d in (1, 3, 2, 0):
            target = ctx_at(x + d, y) if half == 0 else ctx_at(x, y + d)
            added = None
            for entry, part in found:
                term = part * jnp.where(entry == target, 1.0, 0.0)
                added = term if added is None else added + term
            if d == 0:
                kept.append(added)
            else:
                mid[half, d - 1] = added.astype(BF16)
                start(mid_copy(half, d))

    near_copy.wait_recv()
    has_next = jnp.where(me < 15, 1.0, 0.0)
    for half in (0, 1):
        for d in (1, 2, 3):
            mid_copy(half, d).wait_recv()
        rows = halves[half]
        result = own_ref[rows] + near[rows].astype(F32) * has_next + kept[half]
        for d in (1, 2, 3):
            result += back[half, d - 1].astype(F32)
        lat_ref[rows] = result
        every[me, rows] = result.astype(BF16)

    plane_gather(every, x, y, all_s, all_r)

    weight = None
    for b in range(0, 16, 4):
        xt = jnp.concatenate([xt_ref[b + i] for i in range(4)], axis=1)
        gt = jnp.concatenate([every[b + i] for i in range(4)], axis=1)
        term = lax.dot_general(xt, gt, NT, preferred_element_type=F32)
        weight = term if weight is None else weight + term
    rows = weight.shape[0] // n_dp
    for i in range(n_dp):
        pieces[i, :rows] = weight[i * rows : (i + 1) * rows].astype(BF16)
        pieces[i, rows:] = jnp.zeros((pieces.shape[1] - rows, W), BF16)

    def dp_copy(d):
        to = (dp + d) % n_dp
        return remote(pieces.at[to], arrived.at[d - 1], dp_s.at[d - 1], dp_r.at[d - 1], {"dp": to})

    def sum_copy(d, owner):
        return remote(total, totals.at[owner], sum_s.at[d - 1], sum_r.at[d - 1], {"dp": (dp + d) % n_dp})

    for d in range(1, n_dp):
        start(dp_copy(d))
    added = pieces[dp].astype(F32)
    for d in range(1, n_dp):
        dp_copy(d).wait_recv()
        added += arrived[d - 1].astype(F32)
    total[...] = added.astype(BF16)
    for d in range(1, n_dp):
        start(sum_copy(d, dp))
    totals[dp] = total[...]
    for d in range(1, n_dp):
        sum_copy(d, (dp + n_dp - d) % n_dp).wait_recv()
    for i in range(n_dp):
        w_ref[i * rows : (i + 1) * rows] = totals[i].astype(F32)[:rows]
    for c in started:
        c.wait_send()


def tail(rows_list, own, parts, xt, n_dp):
    cols = xt.shape[1]
    vmem = pl.BlockSpec(memory_space=pltpu.VMEM)
    pad = (cols // n_dp + 15) // 16 * 16
    dma = pltpu.SemaphoreType.DMA
    return pl.pallas_call(
        tail_kernel,
        out_shape=[jax.ShapeDtypeStruct((W, TOK), F32), jax.ShapeDtypeStruct((cols, W), F32)],
        in_specs=[pl.BlockSpec(memory_space=pltpu.SMEM), vmem, vmem, vmem],
        out_specs=[vmem, vmem],
        scratch_shapes=[
            pltpu.VMEM((2, 3, 2, HALF, TOK), BF16),
            pltpu.VMEM((2, 3, HALF, TOK), BF16),
            pltpu.VMEM((2, 3, HALF, TOK), BF16),
            pltpu.VMEM((W, TOK), BF16),
            pltpu.VMEM((16, W, TOK), BF16),
            pltpu.VMEM((n_dp, pad, W), BF16),
            pltpu.VMEM((n_dp - 1, pad, W), BF16),
            pltpu.VMEM((pad, W), BF16),
            pltpu.VMEM((n_dp, pad, W), BF16),
            dma((2, 3)), dma((2, 3)), dma((2, 3)), dma((2, 3)), dma, dma,
            dma((30,)), dma((30,)), dma((n_dp - 1,)), dma((n_dp - 1,)), dma((n_dp - 1,)), dma((n_dp - 1,)),
        ],
        compiler_params=pltpu.CompilerParams(
            collective_id=1, has_side_effects=True, vmem_limit_bytes=48 * 2**20
        ),
        name="tail",
    )(rows_list, own, parts, xt)


def per_device(queries, latents, out_grad, layer_input, block_list):
    own_block = lax.axis_index("ctx")
    n_dp = lax.axis_size("dp")
    row_list = lax.dynamic_index_in_dim(block_list[0], own_block, 0, keepdims=False)
    every = gather_latents(latents.transpose(0, 2, 1))
    inputs_t = layer_input[0].T.reshape(16, -1, TOK)
    xt = lax.all_to_all(inputs_t, "ctx", 0, 0, tiled=True)
    own, parts = attention(row_list, every, queries[0].transpose(1, 2, 0), out_grad[0])
    lat_t, weight_grad = tail(block_list[0], own, parts, xt, n_dp)
    return (lat_t.T[None], weight_grad)


def solution(mesh):
    placed = (
        P("dp", "ctx", None, None),
        P("dp", "ctx", None),
        P("dp", "ctx", None, None),
        P("dp", "ctx", None),
        P("dp", None, None),
    )
    return jax.shard_map(
        per_device,
        mesh=mesh,
        in_specs=placed,
        out_specs=(P("dp", "ctx", None), P("ctx", None)),
        check_vma=False,
    )
```

time: 453 us -> 142 us (0.31)
  waiting for transfers between devices: 280 us -> 0.01 us
  Pallas kernels: 0 us -> 127 us
  matrix products: 67.6 us -> 0 us
  local copies, waits for them, and re-layouts: 71.1 us -> 6.87 us
  other arithmetic: 18.1 us -> 0 us
  between operations: 13.8 us -> 0.68 us
  starting transfers between devices: 0.12 us -> 7.72 us
    psum x1 -> x0, waiting for transfers between devices: 168 us -> none  [per_device(): summed = lax.psum(token_inner(own_input, grad_b), ('dp', 'ctx'))]
    pallas_call x0 -> x3, Pallas kernels: none -> 127 us  [the longest x1 58.3 us: tail(): pl.pallas_call(tail_kernel, out_shape=[jax.ShapeDtypeStruct((W, TOK), F32...]
    reduce_scatter x1 -> x0, waiting for transfers between devices: 77.1 us -> none  [per_device(): lax.psum_scatter(spread.reshape(blocks * block_len, width), 'ctx', scatte...]
    dot_general x18 -> x0, matrix products: 67.6 us -> none  [the longest x4 27.4 us: block_grads(): key_grad = jnp.dot(dscore.T, query_rows, preferred_element_type=jnp.float32)]
    all_gather x1 -> x0, waiting for transfers between devices: 34.4 us -> none  [per_device(): lax.all_gather(own_latents, 'ctx', axis=0, tiled=True)]
    unnamed x11 -> x8, local copies, waits for them, and re-layouts: 23.8 us -> 3.58 us
    reshape x9 -> x0, local copies, waits for them, and re-layouts: 17.6 us -> none  [the longest x4 9.92 us: group_step(): lax.dynamic_slice_in_dim(own_grad, index * group, group, 1)]
    dynamic_slice x9 -> x1, local copies, waits for them, and re-layouts: 16.9 us -> 0.78 us  [per_device(): lax.dynamic_index_in_dim(block_list[0], own_block, 0, keepdims=False)]
  transfers between devices with their start and end apart: 3 -> 1, of which waited for: 3 -> 0; matrix products, arithmetic and copies ran while one was open for 4% -> 1% of each run, Pallas kernels for 0% -> 48%
where the time goes in v1:
time: 142 us
  Pallas kernels  127 us (89%)
  starting transfers between devices  7.72 us (5%)
  local copies, waits for them, and re-layouts  6.87 us (5%)
    pallas_call x1, Pallas kernels, tail(): pl.pallas_call(tail_kernel, out_shape=[jax.ShapeDtypeStruct((W, TOK), F32...  58.3 us
    pallas_call x1, Pallas kernels, attention(): pl.pallas_call(functools.partial(attn_kernel, heads, sub), grid_spec=pltp...  34.8 us
    pallas_call x1, Pallas kernels, gather_latents(): pl.pallas_call(gather_kernel, out_shape=jax.ShapeDtypeStruct((16, W, TOK)...  33.6 us
    all_to_all x1, starting transfers between devices, per_device(): xt = lax.all_to_all(inputs_t, 'ctx', 0, 0, tiled=True)  7.72 us
    unnamed x8, local copies, waits for them, and re-layouts  3.58 us
  transfers between devices with their start and end apart: 1, of which 0 were waited for; matrix products, arithmetic and copies ran while one was open for 1% of the time, Pallas kernels for 48%

profile of v1, /device:TPU:1, one launch (start us, length us, event | category | flops | bytes accessed | tf_op | source)
XLA Modules:
  0.0 142.0 jit_solution(2606953512397819071)
XLA Ops:
  0.6 2.4 %copy.7 = bf16[5120,128]{1,0:T(8,128)(2,1)} copy(bf16[5120,128]{0,1:T(8,128)(2,1)} %bitcast.14) | data formatting | bytes 2621440 | tf_op jit(solution)/shard_map/transpose | solution.py:341
  3.1 0.0 copy-start.2
  3.1 7.7 %all-to-all-start = ((bf16[16,320,128]{2,1,0:T(8,128)(2,1)}), bf16[16,320,128]{2,1,0:T(8,128)(2,1)S(1)}, u32[]{:S(2)}, u32[]{:S(2)}) async-start(bf16[16,320,128]{2,1,0:T(8,128)(2,1)} %bitcast.7), calls=%async_computation | async-start | bytes 2621440 | tf_op jit(solution)/shard_map/all_to_all | solution.py:342
  10.8 33.6 %gather_latents.1.k0.k1.k2.k3 = bf16[16,576,128]{2,1,0:T(8,128)(2,1)} custom-call(bf16[1,576,128]{2,1,0:T(8,128)(2,1)} %bitcast.15), custom_call_target="tpu_custom_call" | custom-call | tf_op jit(solution)/shard_map/gather_latents/pallas_call | solution.py:92
  44.4 0.0 copy-done.2
  44.5 0.8 dynamic-slice_reduce_fusion.lst
  45.2 0.1 copy.8.lst
  45.3 34.8 %attention.1 = (f32[576,128]{1,0:T(8,128)}, bf16[3,576,128]{2,1,0:T(8,128)(2,1)}) custom-call(s32[4]{0:T(128)} %dynamic-slice_reduce_fusion.lst, bf16[16,576,128]{2,1,0:T(8,128)(2,1)} %gather_latents.1.k0.k1.k2.k3, bf16[16,576,128]{2,1,0:T(8,128)(2,1)} %gather_latents.1.k0.k1.k2.k3, bf16[16,576,128]{2,1,0:T(8,128)(2,1)} %gather_latents.1.k0.k1.k2.k3, ...), custom_call_target="tpu_custom_call" | custom-call | flops 22000001024 | bytes 20000000 | tf_op jit(solution)/shard_map/attention/pallas_call | solution.py:160
  80.1 0.0 all-to-all-done.xt_ref
  80.1 0.0 copy-start
  80.1 1.0 copy-done
  81.1 0.0 copy-start.1
  81.1 1.0 copy-done.1
  82.1 58.3 %tail.1 = (f32[576,128]{1,0:T(8,128)S(1)}, f32[320,576]{1,0:T(8,128)S(1)}) custom-call(s32[16,4]{1,0:T(8,128)S(1)} %copy.8.lst, f32[576,128]{1,0:T(8,128)S(1)} %copy-done.1, bf16[3,576,128]{2,1,0:T(8,128)(2,1)S(1)} %copy-done, bf16[16,320,128]{2,1,0:T(8,128)(2,1)S(1)} %all-to-all-done.xt_ref), custom_call_target="tpu_custom_call" | custom-call | tf_op jit(solution)/shard_map/tail/pallas_call | solution.py:311
  140.4 0.7 copy.11
  141.1 0.9 copy.12
Async XLA Ops:
  3.1 41.4 %copy-start.2 = (s32[1,16,4]{1,2,0:T(4,128)S(1)}, s32[1,16,4]{1,2,0:T(4,128)}, u32[]{:S(2)}) copy-start(s32[1,16,4]{1,2,0:T(4,128)} %param.9) | copy-start | bytes 772
  3.1 77.1 %all-to-all-start = ((bf16[16,320,128]{2,1,0:T(8,128)(2,1)}), bf16[16,320,128]{2,1,0:T(8,128)(2,1)S(1)}, u32[]{:S(2)}, u32[]{:S(2)}) async-start(bf16[16,320,128]{2,1,0:T(8,128)(2,1)} %bitcast.7), calls=%async_computation | async-start | bytes 2621440 | tf_op jit(solution)/shard_map/all_to_all | solution.py:342
  80.1 1.0 copy-start
  81.1 1.0 copy-start.1

commit v2 on v0

v2 whole, which is shorter than its diff:
```python
import jax
import jax.numpy as jnp
from jax import lax
from jax.experimental import pallas as pl
from jax.experimental.pallas import tpu as pltpu
from jax.sharding import PartitionSpec as P

R = 512
W = 576
HALF = 288
TOK = 128
SLOTS = 4
SIDE = 4
HEADS = 16
SUB = 4
SCALE = 192 ** -0.5
LOG2E = 1.4426950408889634
NT = (((1,), (1,)), ((), ()))
MESH = pl.DeviceIdType.MESH
F32 = jnp.float32
BF16 = jnp.bfloat16
TOP, LOW = pl.ds(0, HALF), pl.ds(HALF, HALF)


def place():
    me = lax.axis_index("ctx")
    return me, me // SIDE, me % SIDE


def ctx_at(x, y):
    return (x % SIDE) * SIDE + y % SIDE


def remote(src, dst, send, recv, device):
    return pltpu.make_async_remote_copy(
        src_ref=src, dst_ref=dst, send_sem=send, recv_sem=recv, device_id=device, device_id_type=MESH
    )


def greet(devices):
    barrier = pltpu.get_barrier_semaphore()
    for device in devices:
        pl.semaphore_signal(barrier, inc=1, device_id=device, device_id_type=MESH)
    pl.semaphore_wait(barrier, len(devices))


def line_peers(x, y):
    return [{"ctx": ctx_at(x + d, y)} for d in (1, 2, 3)] + [{"ctx": ctx_at(x, y + d)} for d in (1, 2, 3)]


class Gather:
    def __init__(self, every, x, y, send, recv, started):
        self.every, self.x, self.y, self.send, self.recv, self.started = every, x, y, send, recv, started

    def copy(self, bx, by, rows, k, dx, dy):
        piece = self.every.at[ctx_at(bx, by), rows]
        device = {"ctx": ctx_at(self.x + dx, self.y + dy)}
        return remote(piece, piece, self.send.at[k], self.recv.at[k], device)

    def start(self, *args):
        c = self.copy(*args)
        c.start()
        self.started.append(c)

    def first(self):
        x, y = self.x, self.y
        for d in (1, 3, 2):
            self.start(x, y, TOP, d - 1, d, 0)
            self.start(x, y, LOW, 3 + d - 1, 0, d)

    def forward(self, j):
        x, y = self.x, self.y
        if j > 0:
            self.copy(x - j, y, TOP, j - 1, j, 0).wait_recv()
            self.copy(x, y - j, LOW, 3 + j - 1, 0, j).wait_recv()
        for d in (1, 3, 2):
            self.start(x - j, y, TOP, 6 + 3 * j + d - 1, 0, d)
            self.start(x, y - j, LOW, 18 + 3 * j + d - 1, d, 0)

    def finish(self):
        x, y = self.x, self.y
        for j in range(SIDE):
            for d in (1, 2, 3):
                self.copy(x - j, y - d, TOP, 6 + 3 * j + d - 1, 0, d).wait_recv()
                self.copy(x - d, y - j, LOW, 18 + 3 * j + d - 1, d, 0).wait_recv()


def kernel(
    lst, lat, qt, do, inp, lat_ref, w_ref,
    q_v, stage, d_v, every, prev, k_v, s_v, dp_v, acc, parts, raw, mid, back, near, gbuf, xa, xt,
    cs0, cs1, cr0, cr1, ys0, ys1, yr0, yr1, zr0, zr1, fin0, fin1,
    q_s, do_s, own_s, all_s, all_r, prev_s, prev_r, x_s, x_r, xo_s, raw_s, raw_r, mid_s, mid_r, near_s, near_r,
    g_s, g_r, c_s, c_r, y_s, y_r, z_s, z_r, f_s, f_r,
):
    me, x, y = place()
    dp = lax.axis_index("dp")
    n_dp = lax.axis_size("dp")
    core, z = dp % 2, dp // 2
    twin = {"dp": dp + 1 - 2 * core}
    after, before = {"ctx": (me + 1) % 16}, {"ctx": (me + 15) % 16}
    n_heads = q_v.shape[0]
    steps = n_heads // HEADS
    quarter = xa.shape[2]
    started = []

    def start(c):
        c.start()
        started.append(c)

    def do_load(i):
        return pltpu.make_async_copy(do.at[:, pl.ds(i * HEADS, HEADS)], stage.at[i % 2], do_s.at[i % 2])

    def q_load(i):
        part = pl.ds(i * HEADS, HEADS)
        return pltpu.make_async_copy(qt.at[part], q_v.at[part], q_s.at[i])

    own_load = pltpu.make_async_copy(lat.at[0], every.at[me], own_s)
    own_load.start()
    do_load(0).start()
    q_load(0).start()
    do_load(1).start()
    for i in range(1, steps):
        q_load(i).start()
    x_own = pltpu.make_async_copy(
        inp.at[:, pl.ds(pl.multiple_of(x * quarter, 128), quarter)], xa.at[0], xo_s
    )
    greet(
        line_peers(x, y) + [after, before, twin] + [{"dp": (dp + 2 * d) % n_dp} for d in range(1, n_dp // 2)]
    )
    own_load.wait()
    prev_copy = remote(every.at[me], prev, prev_s, prev_r, after)
    start(prev_copy)
    gather = Gather(every, x, y, all_s, all_r, started)
    gather.first()
    x_own.start()

    k_v[:TOK] = every[me].T
    prev_copy.wait_recv()
    k_v[TOK : 2 * TOK] = prev[...].T
    gather.forward(0)

    def columns(at):
        return (
            jnp.concatenate([q_v[at * SUB + i] for i in range(SUB)], axis=1),
            d_v[pl.ds(at * SUB, SUB)].reshape(SUB * TOK, R),
        )

    def products(keys, qc, dc):
        return (
            jnp.dot(keys, qc, preferred_element_type=F32),
            lax.dot_general(keys[:, :R], dc, NT, preferred_element_type=F32),
        )

    per = HEADS // SUB
    for i in range(steps):
        do_load(i).wait()
        q_load(i).wait()
        d_v[i * HEADS : (i + 1) * HEADS] = jnp.swapaxes(stage[i % 2], 0, 1)
        if i + 2 < steps:
            do_load(i + 2).start()

        window = k_v[: 2 * TOK]
        for k in range(per):
            at = i * per + k
            s_v[at], dp_v[at] = products(window, *columns(at))
        if i < 2:
            for j in ((1, 3), (2,))[i]:
                gather.forward(j)
    gather.finish()

    def x_copy(d):
        to = (x + d) % SIDE
        return remote(
            inp.at[:, pl.ds(pl.multiple_of(to * quarter, 128), quarter)],
            xa.at[d], x_s.at[d - 1], x_r.at[d - 1], {"ctx": ctx_at(x + d, y)},
        )

    for d in (1, 3, 2):
        start(x_copy(d))

    for e in (2, 3):
        k_v[e * TOK : (e + 1) * TOK] = every[jnp.maximum(lst[me, e], 0)].T
    acc[...] = jnp.zeros_like(acc)
    key_at = lax.broadcasted_iota(jnp.int32, (TOK, TOK), 0)
    tok_at = lax.broadcasted_iota(jnp.int32, (TOK, TOK), 1)
    causal = jnp.concatenate([key_at <= tok_at] * SUB, axis=1)
    away = [None] + [jnp.where(lst[me, e] >= 0, 0.0, jnp.inf) for e in range(1, SLOTS)]
    c = SCALE * LOG2E

    def softmax(at):
        qc, dc = columns(at)
        s_far, dp_far = products(k_v[2 * TOK :], qc, dc)
        ss = [s_v[at, :TOK], s_v[at, TOK:], s_far[:TOK], s_far[TOK:]]
        dprob = jnp.concatenate([dp_v[at], dp_far], axis=0)
        ss[0] = jnp.where(causal, ss[0], -jnp.inf)
        top = jnp.max(ss[0], axis=0, keepdims=True)
        for e in range(1, SLOTS):
            top = jnp.maximum(top, jnp.max(ss[e], axis=0, keepdims=True) - away[e])
        mc = top * c
        p = jnp.concatenate(
            [jnp.exp2(ss[e] * c - (mc if e == 0 else mc + away[e])) for e in range(SLOTS)], axis=0
        )
        inv = 1.0 / jnp.sum(p, axis=0, keepdims=True)
        delta = jnp.sum(p * dprob, axis=0, keepdims=True) * inv
        probs = p * inv
        return qc, dc, probs.astype(BF16), (probs * (dprob - delta)).astype(BF16)

    def grads(qc, dc, pb, ds):
        kg = lax.dot_general(ds, qc, NT, preferred_element_type=F32) * SCALE
        vg = jnp.dot(pb, dc, preferred_element_type=F32)
        acc[:, :R] += kg[:, :R] + vg
        acc[:, R:] += kg[:, R:]

    def attend(i, carry):
        held = None
        for k in range(per):
            fresh = softmax(i * per + k)
            if held is not None:
                grads(*held)
            held = fresh
        grads(*held)
        return carry

    lax.fori_loop(0, steps, attend, 0)

    halves = (TOP, LOW)

    def raw_copy(half, d):
        return remote(
            parts.at[pl.ds(1, 2), halves[half]], raw.at[half, d - 1], raw_s.at[half, d - 1], raw_r.at[half, d - 1],
            {"ctx": ctx_at(x, y + d) if half == 0 else ctx_at(x + d, y)},
        )

    for e in (2, 3):
        parts[e - 1] = acc[e * TOK : (e + 1) * TOK].T.astype(BF16)
    for d in (1, 3, 2):
        for half in (0, 1):
            start(raw_copy(half, d))
    parts[0] = acc[TOK : 2 * TOK].T.astype(BF16)
    near_copy = remote(parts.at[0], near, near_s, near_r, before)
    start(near_copy)

    x_own.wait()
    for d in range(SIDE):
        if d > 0:
            x_copy(d).wait_recv()
        xt[:, d * TOK : (d + 1) * TOK] = xa[d].T
    lat_ref[...] = acc[:TOK].T

    def mid_copy(half, d):
        return remote(
            mid.at[half, d - 1], back.at[half, d - 1], mid_s.at[half, d - 1], mid_r.at[half, d - 1],
            {"ctx": ctx_at(x + d, y) if half == 0 else ctx_at(x, y + d)},
        )

    for half in (0, 1):
        found = []
        for d in range(SIDE):
            src = ctx_at(x, y - d) if half == 0 else ctx_at(x - d, y)
            if d > 0:
                raw_copy(half, d).wait_recv()
            for e in range(2):
                part = parts[1 + e, halves[half]] if d == 0 else raw[half, d - 1, e]
                found.append((lst[src, 2 + e], part.astype(F32)))
        for d in (1, 3, 2, 0):
            target = ctx_at(x + d, y) if half == 0 else ctx_at(x, y + d)
            added = None
            for entry, part in found:
                term = part * jnp.where(entry == target, 1.0, 0.0)
                added = term if added is None else added + term
            if d == 0:
                lat_ref[halves[half]] += added
            else:
                mid[half, d - 1] = added.astype(BF16)
                start(mid_copy(half, d))

    near_copy.wait_recv()
    has_next = jnp.where(me < 15, 1.0, 0.0)
    for half in (0, 1):
        rows = halves[half]
        result = lat_ref[rows] + near[rows].astype(F32) * has_next
        for d in (1, 2, 3):
            mid_copy(half, d).wait_recv()
            result += back[half, d - 1].astype(F32)
        lat_ref[rows] = result
        gbuf[0, rows] = result.astype(BF16)

    chunks = ((0, 256), (256, W - 256))
    cs, cr, ys, yr = (cs0, cs1), (cr0, cr1), (ys0, ys1), (yr0, yr1)
    zr, fin = (zr0, zr1), (fin0, fin1)

    def g_copy(ch, d):
        rows = pl.ds(*chunks[ch])
        return remote(
            gbuf.at[0, rows], gbuf.at[d, rows], g_s.at[ch, d - 1], g_r.at[ch, d - 1], {"ctx": ctx_at(x + d, y)}
        )

    def c_copy(ch):
        return remote(cs[ch], cr[ch], c_s.at[ch], c_r.at[ch], twin)

    def y_copy(ch, d):
        to = (y + d) % SIDE
        return remote(ys[ch].at[to], yr[ch].at[d - 1], y_s.at[ch, d - 1], y_r.at[ch, d - 1], {"ctx": ctx_at(x, to)})

    def z_copy(ch, d, owner):
        piece = zr[ch].at[owner]
        return remote(piece, piece, z_s.at[ch, d - 1], z_r.at[ch, d - 1], {"dp": (dp + 2 * d) % n_dp})

    def f_copy(ch, owner):
        piece = fin[ch].at[owner]
        return remote(piece, piece, f_s.at[ch], f_r.at[ch], twin)

    part = cs0.shape[1]

    def slot(ch, row, half):
        return s_v.at[(ch * SIDE + row) * 2 + half, pl.ds(0, part), pl.ds(0, chunks[ch][1])]

    n_z = n_dp // 2
    for ch in (0, 1):
        for d in (1, 3, 2):
            start(g_copy(ch, d))
    for ch in (0, 1):
        for d in (1, 2, 3):
            g_copy(ch, d).wait_recv()
        rows = pl.ds(*chunks[ch])
        gt = jnp.concatenate([gbuf[d, rows] for d in range(SIDE)], axis=1)
        weight = lax.dot_general(xt[...], gt, NT, preferred_element_type=F32)
        for i in range(2 * SIDE):
            slot(ch, i // 2, i % 2)[...] = weight[i * part : (i + 1) * part]
        for i in range(SIDE):
            cs[ch][i] = slot(ch, i, 1 - core)[...].astype(BF16)
        start(c_copy(ch))
    for ch in (0, 1):
        c_copy(ch).wait_recv()
        for i in range(SIDE):
            both = slot(ch, i, core)[...] + cr[ch][i].astype(F32)
            slot(ch, i, core)[...] = both
            ys[ch][i] = both.astype(BF16)
        for d in (1, 3, 2):
            start(y_copy(ch, d))
    for ch in (0, 1):
        added = slot(ch, y, core)[...]
        for d in (1, 2, 3):
            y_copy(ch, d).wait_recv()
            added += yr[ch][d - 1].astype(F32)
        zr[ch][z] = added.astype(BF16)
        for d in range(1, n_z):
            start(z_copy(ch, d, z))
    for ch in (0, 1):
        for d in range(1, n_z):
            z_copy(ch, d, (z + n_z - d) % n_z).wait_recv()
        added = zr[ch][0].astype(F32)
        for i in range(1, n_z):
            added += zr[ch][i].astype(F32)
        fin[ch][core] = added
        start(f_copy(ch, core))
    for ch in (0, 1):
        f_copy(ch, 1 - core).wait_recv()
        first, count = chunks[ch]
        for i in (0, 1):
            half_rows = fin[ch].shape[1]
            w_ref[i * half_rows : (i + 1) * half_rows, first : first + count] = fin[ch][i]
    for c in started:
        c.wait_send()


def per_device(queries, latents, out_grad, layer_input, block_list):
    n_dp = lax.axis_size("dp")
    n_z = n_dp // 2
    n_heads = queries.shape[2]
    cols = layer_input.shape[2] // 16
    vmem = pl.BlockSpec(memory_space=pltpu.VMEM)
    hbm = pl.BlockSpec(memory_space=pl.ANY)
    dma = pltpu.SemaphoreType.DMA
    v = pltpu.VMEM
    n0, n1 = 256, W - 256
    part = cols // 2
    lat_t, weight_grad = pl.pallas_call(
        kernel,
        out_shape=[jax.ShapeDtypeStruct((W, TOK), F32), jax.ShapeDtypeStruct((cols, W), F32)],
        in_specs=[pl.BlockSpec(memory_space=pltpu.SMEM), hbm, hbm, hbm, hbm],
        out_specs=[vmem, vmem],
        scratch_shapes=[
            v((n_heads, W, TOK), BF16),
            v((2, TOK, HEADS, R), BF16),
            v((n_heads, TOK, R), BF16),
            v((16, W, TOK), BF16),
            v((W, TOK), BF16),
            v((SLOTS * TOK, W), BF16),
            v((n_heads // SUB, 2 * TOK, SUB * TOK), F32),
            v((n_heads // SUB, 2 * TOK, SUB * TOK), F32),
            v((SLOTS * TOK, W), F32),
            v((3, W, TOK), BF16),
            v((2, 3, 2, HALF, TOK), BF16),
            v((2, 3, HALF, TOK), BF16),
            v((2, 3, HALF, TOK), BF16),
            v((W, TOK), BF16),
            v((SIDE, W, TOK), BF16),
            v((SIDE, TOK, SIDE * cols), BF16),
            v((SIDE * cols, SIDE * TOK), BF16),
            v((SIDE, part, n0), BF16), v((SIDE, part, n1), BF16),
            v((SIDE, part, n0), BF16), v((SIDE, part, n1), BF16),
            v((SIDE, part, n0), BF16), v((SIDE, part, n1), BF16),
            v((3, part, n0), BF16), v((3, part, n1), BF16),
            v((n_z, part, n0), BF16), v((n_z, part, n1), BF16),
            v((2, part, n0), F32), v((2, part, n1), F32),
            dma((n_heads // HEADS,)), dma((2,)), dma, dma((30,)), dma((30,)), dma, dma,
            dma((3,)), dma((3,)), dma, dma((2, 3)), dma((2, 3)), dma((2, 3)), dma((2, 3)), dma, dma,
            dma((2, 3)), dma((2, 3)), dma((2,)), dma((2,)), dma((2, 3)), dma((2, 3)),
            dma((2, n_z - 1)), dma((2, n_z - 1)), dma((2,)), dma((2,)),
        ],
        compiler_params=pltpu.CompilerParams(
            collective_id=0, has_side_effects=True, vmem_limit_bytes=60 * 2**20
        ),
        name="attention_backward",
    )(
        block_list[0],
        latents.transpose(0, 2, 1),
        queries[0].transpose(1, 2, 0),
        out_grad[0],
        layer_input[0],
    )
    return (lat_t.T[None], weight_grad)


def solution(mesh):
    placed = (
        P("dp", "ctx", None, None),
        P("dp", "ctx", None),
        P("dp", "ctx", None, None),
        P("dp", "ctx", None),
        P("dp", None, None),
    )
    return jax.shard_map(
        per_device,
        mesh=mesh,
        in_specs=placed,
        out_specs=(P("dp", "ctx", None), P("ctx", None)),
        check_vma=False,
    )
```

time: 453 us -> 101 us (0.22)
  waiting for transfers between devices: 280 us -> 0 us
  Pallas kernels: 0 us -> 94.4 us
  matrix products: 67.6 us -> 0 us
  local copies, waits for them, and re-layouts: 71.1 us -> 5.14 us
  other arithmetic: 18.1 us -> 0 us
  between operations: 13.8 us -> 0.64 us
    psum x1 -> x0, waiting for transfers between devices: 168 us -> none  [per_device(): summed = lax.psum(token_inner(own_input, grad_b), ('dp', 'ctx'))]
    pallas_call x0 -> x1, Pallas kernels: none -> 94.4 us  [per_device(): pl.pallas_call(kernel, out_shape=[jax.ShapeDtypeStruct((W, TOK), F32), ja...]
    reduce_scatter x1 -> x0, waiting for transfers between devices: 77.1 us -> none  [per_device(): lax.psum_scatter(spread.reshape(blocks * block_len, width), 'ctx', scatte...]
    dot_general x18 -> x0, matrix products: 67.6 us -> none  [the longest x4 27.4 us: block_grads(): key_grad = jnp.dot(dscore.T, query_rows, preferred_element_type=jnp.float32)]
    all_gather x1 -> x0, waiting for transfers between devices: 34.4 us -> none  [per_device(): lax.all_gather(own_latents, 'ctx', axis=0, tiled=True)]
    unnamed x11 -> x2, local copies, waits for them, and re-layouts: 23.8 us -> 3.78 us
    reshape x9 -> x0, local copies, waits for them, and re-layouts: 17.6 us -> none  [the longest x4 9.92 us: group_step(): lax.dynamic_slice_in_dim(own_grad, index * group, group, 1)]
    dynamic_slice x9 -> x0, local copies, waits for them, and re-layouts: 16.9 us -> none  [the longest x4 8.19 us: group_step(): lax.dynamic_slice_in_dim(own_queries, index * group, group, 1)]
  transfers between devices with their start and end apart: 3 -> 0, of which waited for: 3 -> 0; matrix products, arithmetic and copies ran while one was open for 4% -> 0% of each run, Pallas kernels for 0% -> 0%
where the time goes in v2:
time: 101 us; the launch traced here: 100 us
  Pallas kernels  94.4 us (93%)
  local copies, waits for them, and re-layouts  5.14 us (5%)
    pallas_call x1, Pallas kernels, per_device(): pl.pallas_call(kernel, out_shape=[jax.ShapeDtypeStruct((W, TOK), F32), ja...  94.4 us
    unnamed x2, local copies, waits for them, and re-layouts  3.78 us

profile of v2, /device:TPU:1, one launch (start us, length us, event | category | flops | bytes accessed | tf_op | source)
XLA Modules:
  0.0 100.2 jit_solution(7345141099023520023)
XLA Ops:
  0.6 1.4 %copy.7.lst = s32[16,4]{1,0:T(8,128)} copy(s32[16,4]{0,1:T(4,128)} %bitcast.15) | data formatting | bytes 512 | tf_op jit(solution)/shard_map/squeeze | solution.py:417
  2.0 94.4 %attention_backward.1 = (f32[576,128]{1,0:T(8,128)}, f32[320,576]{1,0:T(8,128)}) custom-call(s32[16,4]{1,0:T(8,128)} %copy.7.lst, bf16[1,576,128]{2,1,0:T(8,128)(2,1)} %bitcast.14, bf16[64,576,128]{2,1,0:T(8,128)(2,1)} %bitcast.10, bf16[128,64,512]{2,1,0:T(8,128)(2,1)} %bitcast.11, bf16[128,5120]{1,0:T(8,128)(2,1)} %bitcast.12), custom_call_target="tpu_custom_call" | custom-call | tf_op jit(solution)/shard_map/attention_backward/pallas_call | solution.py:378
  96.4 1.7 %copy.10 = f32[1,128,576]{1,2,0:T(8,128)} copy(f32[1,128,576]{1,2,0:T(8,128)} %bitcast.13) | data formatting | bytes 589824
  98.1 2.1 %copy.11 = f32[320,576]{1,0:T(8,128)} copy(f32[320,576]{1,0:T(8,128)} %get-tuple-element.9) | data formatting | bytes 1474560

commit v3 on v2

v3 whole, which is shorter than its diff:
```python
import jax
import jax.numpy as jnp
from jax import lax
from jax.experimental import pallas as pl
from jax.experimental.pallas import tpu as pltpu
from jax.sharding import PartitionSpec as P

R = 512
W = 576
HALF = 288
TOK = 128
SLOTS = 4
SIDE = 4
HEADS = 16
SUB = 4
SPANS = ((0, 128), (128, 192), (320, 128), (448, 128))
SCALE = 192 ** -0.5
LOG2E = 1.4426950408889634
NT = (((1,), (1,)), ((), ()))
MESH = pl.DeviceIdType.MESH
F32 = jnp.float32
BF16 = jnp.bfloat16
TOP, LOW = pl.ds(0, HALF), pl.ds(HALF, HALF)


def place():
    me = lax.axis_index("ctx")
    return me, me // SIDE, me % SIDE


def ctx_at(x, y):
    return (x % SIDE) * SIDE + y % SIDE


def remote(src, dst, send, recv, device):
    return pltpu.make_async_remote_copy(
        src_ref=src, dst_ref=dst, send_sem=send, recv_sem=recv, device_id=device, device_id_type=MESH
    )


def greet(devices):
    barrier = pltpu.get_barrier_semaphore()
    for device in devices:
        pl.semaphore_signal(barrier, inc=1, device_id=device, device_id_type=MESH)
    pl.semaphore_wait(barrier, len(devices))


def line_peers(x, y):
    return [{"ctx": ctx_at(x + d, y)} for d in (1, 2, 3)] + [{"ctx": ctx_at(x, y + d)} for d in (1, 2, 3)]


def kernel(
    lst, lat, qt, do, inp, lat_ref, w_ref,
    q_v, stage, d_v, line, sel, got, prev, k_v, s_v, dp_v, acc, parts, raw, mid, back, near, gbuf, xa, xt,
    cs, cr, ys, yr, zr, fin,
    q_s, do_s, own_s, line_s, line_r, sel_s, sel_r, prev_s, prev_r, x_s, x_r, xo_s, raw_s, raw_r, mid_s, mid_r, near_s, near_r,
    g_s, g_r, c_s, c_r, y_s, y_r, z_s, z_r, f_s, f_r,
):
    me, x, y = place()
    dp = lax.axis_index("dp")
    n_dp = lax.axis_size("dp")
    core, z = dp % 2, dp // 2
    twin = {"dp": dp + 1 - 2 * core}
    after, before = {"ctx": (me + 1) % 16}, {"ctx": (me + 15) % 16}
    n_heads = q_v.shape[0]
    steps = n_heads // HEADS
    quarter = xa.shape[2]
    started = []

    def start(c):
        c.start()
        started.append(c)

    def do_load(i):
        return pltpu.make_async_copy(do.at[:, pl.ds(i * HEADS, HEADS)], stage.at[i % 2], do_s.at[i % 2])

    def q_load(i):
        part = pl.ds(i * HEADS, HEADS)
        return pltpu.make_async_copy(qt.at[part], q_v.at[part], q_s.at[i])

    halves = (TOP, LOW)
    chunks = ((0, 256), (256, W - 256))
    mine = (line.at[0, x], line.at[1, y])
    own_loads = [pltpu.make_async_copy(lat.at[0, halves[h]], mine[h], own_s.at[h]) for h in (0, 1)]
    for load in own_loads:
        load.start()
    do_load(0).start()
    q_load(0).start()
    do_load(1).start()
    for i in range(1, steps):
        q_load(i).start()
    x_own = pltpu.make_async_copy(
        inp.at[:, pl.ds(pl.multiple_of(x * quarter, 128), quarter)], xa.at[0], xo_s
    )
    greet(
        line_peers(x, y) + [after, before, twin] + [{"dp": (dp + 2 * d) % n_dp} for d in range(1, n_dp // 2)]
    )
    for load in own_loads:
        load.wait()

    def along(half, d):
        return {"ctx": ctx_at(x + d, y) if half == 0 else ctx_at(x, y + d)}

    def across(half, d):
        return along(1 - half, d)

    def line_copy(half, d):
        return remote(mine[half], mine[half], line_s.at[half, d - 1], line_r.at[half, d - 1], along(half, d))

    def line_wait(half, d):
        slot = line.at[0, (x + SIDE - d) % SIDE] if half == 0 else line.at[1, (y + SIDE - d) % SIDE]
        remote(slot, slot, line_s.at[half, d - 1], line_r.at[half, d - 1], along(half, d)).wait_recv()

    def prev_copy(half):
        return remote(mine[half], prev.at[half], prev_s.at[half], prev_r.at[half], after)

    start(prev_copy(0))

    @pl.when(y == SIDE - 1)
    def _():
        prev_copy(1).start()

    for d in (1, 3, 2):
        for half in (0, 1):
            start(line_copy(half, d))
    x_own.start()

    k_v[:TOK] = jnp.concatenate([line[0, x], line[1, y]], axis=0).T
    prev_copy(0).wait_recv()
    line_wait(1, 1)

    @pl.when(y == 0)
    def _():
        prev_copy(1).wait_recv()
        k_v[TOK : 2 * TOK] = jnp.concatenate([prev[0], prev[1]], axis=0).T

    @pl.when(y > 0)
    def _():
        k_v[TOK : 2 * TOK] = jnp.concatenate([prev[0], line[1, (y + SIDE - 1) % SIDE]], axis=0).T

    def listed(device, e):
        block = jnp.maximum(lst[2 + e, device], 0)
        return block >> 2, block & 3

    def sel_copy(half, d):
        return remote(
            sel.at[half, d - 1], got.at[half, d], sel_s.at[half, d - 1], sel_r.at[half, d - 1], across(half, d)
        )

    def pass_on():
        for half in (0, 1):
            for d in (1, 2, 3):
                if half == 0 or d > 1:
                    line_wait(half, d)
        for d in (1, 3, 2, 0):
            for half in (0, 1):
                for e in (0, 1):
                    wanted = listed(across(half, d)["ctx"], e)[half]
                    if d == 0:
                        got[half, 0, e] = line[half, wanted]
                    else:
                        sel[half, d - 1, e] = line[half, wanted]
                if d > 0:
                    start(sel_copy(half, d))

    def columns(at):
        return (
            jnp.concatenate([q_v[at * SUB + i] for i in range(SUB)], axis=1),
            d_v[pl.ds(at * SUB, SUB)].reshape(SUB * TOK, R),
        )

    def products(keys, qc, dc):
        return (
            jnp.dot(keys, qc, preferred_element_type=F32),
            lax.dot_general(keys[:, :R], dc, NT, preferred_element_type=F32),
        )

    per = HEADS // SUB
    for i in range(steps):
        do_load(i).wait()
        q_load(i).wait()
        d_v[i * HEADS : (i + 1) * HEADS] = jnp.swapaxes(stage[i % 2], 0, 1)
        if i + 2 < steps:
            do_load(i + 2).start()

        window = k_v[: 2 * TOK]
        for k in range(per):
            at = i * per + k
            s_v[at], dp_v[at] = products(window, *columns(at))
        if i == 0:
            pass_on()
    for half in (0, 1):
        for d in (1, 2, 3):
            sel_copy(half, d).wait_recv()

    def x_copy(d):
        to = (x + d) % SIDE
        return remote(
            inp.at[:, pl.ds(pl.multiple_of(to * quarter, 128), quarter)],
            xa.at[d], x_s.at[d - 1], x_r.at[d - 1], {"ctx": ctx_at(x + d, y)},
        )

    for d in (1, 3, 2):
        start(x_copy(d))

    for e in (0, 1):
        bx, by = listed(me, e)
        k_v[(2 + e) * TOK : (3 + e) * TOK] = jnp.concatenate(
            [got[0, (y - by) & 3, e], got[1, (x - bx) & 3, e]], axis=0
        ).T
    acc[...] = jnp.zeros_like(acc)
    key_at = lax.broadcasted_iota(jnp.int32, (TOK, TOK), 0)
    tok_at = lax.broadcasted_iota(jnp.int32, (TOK, TOK), 1)
    causal = jnp.concatenate([key_at <= tok_at] * SUB, axis=1)
    away = [None] + [jnp.where(lst[e, me] >= 0, 0.0, jnp.inf) for e in range(1, SLOTS)]
    c = SCALE * LOG2E

    def softmax(at):
        qc, dc = columns(at)
        s_far, dp_far = products(k_v[2 * TOK :], qc, dc)
        ss = [s_v[at, :TOK], s_v[at, TOK:], s_far[:TOK], s_far[TOK:]]
        dprob = jnp.concatenate([dp_v[at], dp_far], axis=0)
        ss[0] = jnp.where(causal, ss[0], -jnp.inf)
        top = jnp.max(ss[0], axis=0, keepdims=True)
        for e in range(1, SLOTS):
            top = jnp.maximum(top, jnp.max(ss[e], axis=0, keepdims=True) - away[e])
        mc = top * c
        p = jnp.concatenate(
            [jnp.exp2(ss[e] * c - (mc if e == 0 else mc + away[e])) for e in range(SLOTS)], axis=0
        )
        inv = 1.0 / jnp.sum(p, axis=0, keepdims=True)
        delta = jnp.sum(p * dprob, axis=0, keepdims=True) * inv
        probs = p * inv
        dscore = probs * (dprob - delta)
        s_v[at] = probs[: 2 * TOK]
        dp_v[at] = dscore[: 2 * TOK]
        return qc, dc, probs[2 * TOK :].astype(BF16), dscore[2 * TOK :].astype(BF16)

    def grads(qc, dc, pb, ds):
        kg = lax.dot_general(ds, qc, NT, preferred_element_type=F32) * SCALE
        vg = jnp.dot(pb, dc, preferred_element_type=F32)
        acc[2 * TOK :, :R] += kg[:, :R] + vg
        acc[2 * TOK :, R:] += kg[:, R:]

    def attend(i, carry):
        held = None
        for k in range(per):
            fresh = softmax(i * per + k)
            if held is not None:
                grads(*held)
            held = fresh
        grads(*held)
        return carry

    lax.fori_loop(0, steps, attend, 0)

    def window_grads(first, count):
        values = min(count, R - first)

        def step(i, carry):
            ats = [i * per + k for k in range(per)]
            ds = jnp.concatenate([dp_v[at].astype(BF16) for at in ats], axis=1)
            pb = jnp.concatenate([s_v[at].astype(BF16) for at in ats], axis=1)
            qc = jnp.concatenate([q_v[i * HEADS + h, first : first + count] for h in range(HEADS)], axis=1)
            dc = d_v[pl.ds(i * HEADS, HEADS), :, first : first + values].reshape(HEADS * TOK, values)
            kg = lax.dot_general(ds, qc, NT, preferred_element_type=F32) * SCALE
            vg = jnp.dot(pb, dc, preferred_element_type=F32)
            acc[: 2 * TOK, first : first + values] += kg[:, :values] + vg
            if values < count:
                acc[: 2 * TOK, first + values : first + count] += kg[:, values:]
            return carry

        lax.fori_loop(0, steps, step, 0)

    def raw_copy(half, d):
        return remote(
            parts.at[pl.ds(1, 2), halves[half]], raw.at[half, d - 1], raw_s.at[half, d - 1], raw_r.at[half, d - 1],
            across(half, d),
        )

    for e in (2, 3):
        parts[e - 1] = acc[e * TOK : (e + 1) * TOK].T.astype(BF16)
    for d in (1, 3, 2):
        for half in (0, 1):
            start(raw_copy(half, d))

    def near_copy(ch):
        rows = pl.ds(*chunks[ch])
        return remote(parts.at[0, rows], near.at[rows], near_s.at[ch], near_r.at[ch], before)

    for ch in (0, 1):
        first, count = chunks[ch]
        window_grads(first, count)
        parts[0, first : first + count] = acc[TOK : 2 * TOK, first : first + count].T.astype(BF16)
        start(near_copy(ch))

    x_own.wait()
    for d in range(SIDE):
        if d > 0:
            x_copy(d).wait_recv()
        xt[:, d * TOK : (d + 1) * TOK] = xa[d].T
    lat_ref[...] = acc[:TOK].T

    def mid_copy(half, d):
        return remote(
            mid.at[half, d - 1], back.at[half, d - 1], mid_s.at[half, d - 1], mid_r.at[half, d - 1],
            along(half, d),
        )

    for half in (0, 1):
        found = []
        for d in range(SIDE):
            src = ctx_at(x, y - d) if half == 0 else ctx_at(x - d, y)
            if d > 0:
                raw_copy(half, d).wait_recv()
            for e in range(2):
                part = parts[1 + e, halves[half]] if d == 0 else raw[half, d - 1, e]
                found.append((lst[2 + e, src], part.astype(F32)))
        for d in (1, 3, 2, 0):
            target = ctx_at(x + d, y) if half == 0 else ctx_at(x, y + d)
            added = None
            for entry, part in found:
                term = part * jnp.where(entry == target, 1.0, 0.0)
                added = term if added is None else added + term
            if d == 0:
                lat_ref[halves[half]] += added
            else:
                mid[half, d - 1] = added.astype(BF16)
                start(mid_copy(half, d))

    for ch in (0, 1):
        near_copy(ch).wait_recv()
    has_next = jnp.where(me < 15, 1.0, 0.0)
    for half in (0, 1):
        rows = halves[half]
        result = lat_ref[rows] + near[rows].astype(F32) * has_next
        for d in (1, 2, 3):
            mid_copy(half, d).wait_recv()
            result += back[half, d - 1].astype(F32)
        lat_ref[rows] = result
        gbuf[0, rows] = result.astype(BF16)

    spans = SPANS

    def g_copy(ch, d):
        rows = pl.ds(*spans[ch])
        return remote(gbuf.at[0, rows], gbuf.at[d, rows], g_s.at[ch, d - 1], g_r.at[ch, d - 1], along(0, d))

    def c_copy(ch):
        return remote(cs[ch], cr[ch], c_s.at[ch], c_r.at[ch], twin)

    def y_copy(ch, d):
        return remote(ys[ch].at[(y + d) % SIDE], yr[ch].at[d - 1], y_s.at[ch, d - 1], y_r.at[ch, d - 1], along(1, d))

    def z_copy(ch, d, owner):
        piece = zr[ch].at[owner]
        return remote(piece, piece, z_s.at[ch, d - 1], z_r.at[ch, d - 1], {"dp": (dp + 2 * d) % n_dp})

    def f_copy(ch, owner):
        piece = fin[ch].at[owner]
        return remote(piece, piece, f_s.at[ch], f_r.at[ch], twin)

    n_z = n_dp // 2
    part = fin[0].shape[1]

    def slot(ch, row, half):
        at, wide = divmod(ch, 2)
        return dp_v.at[at * 2 * SIDE + row * 2 + half, pl.ds(0, part), pl.ds(256 * wide, cs[ch].shape[2])]

    def multiply(ch):
        for d in (1, 2, 3):
            g_copy(ch, d).wait_recv()
        gt = jnp.concatenate([gbuf[d, pl.ds(*spans[ch])] for d in range(SIDE)], axis=1)
        spare = cs[ch].shape[2] - gt.shape[0]
        if spare:
            gt = jnp.concatenate([gt, jnp.zeros((spare, gt.shape[1]), BF16)], axis=0)
        weight = lax.dot_general(xt[...], gt, NT, preferred_element_type=F32)
        for i in range(2 * SIDE):
            slot(ch, i // 2, i % 2)[...] = weight[i * part : (i + 1) * part]
        for i in range(SIDE):
            cs[ch][i] = slot(ch, i, 1 - core)[...].astype(BF16)
        start(c_copy(ch))

    def add_core(ch):
        c_copy(ch).wait_recv()
        for i in range(SIDE):
            both = slot(ch, i, core)[...] + cr[ch][i].astype(F32)
            slot(ch, i, core)[...] = both
            ys[ch][i] = both.astype(BF16)
        for d in (1, 3, 2):
            start(y_copy(ch, d))

    def add_y(ch):
        added = slot(ch, y, core)[...]
        for d in (1, 2, 3):
            y_copy(ch, d).wait_recv()
            added += yr[ch][d - 1].astype(F32)
        zr[ch][z] = added.astype(BF16)
        for d in range(1, n_z):
            start(z_copy(ch, d, z))

    def add_z(ch):
        for d in range(1, n_z):
            z_copy(ch, d, (z + n_z - d) % n_z).wait_recv()
        added = zr[ch][0].astype(F32)
        for i in range(1, n_z):
            added += zr[ch][i].astype(F32)
        fin[ch][core] = added
        start(f_copy(ch, core))

    def put(ch):
        f_copy(ch, 1 - core).wait_recv()
        first, count = spans[ch]
        for i in (0, 1):
            w_ref[i * part : (i + 1) * part, first : first + count] = fin[ch][i, :, :count]

    for ch in range(len(spans)):
        for d in (1, 3, 2):
            start(g_copy(ch, d))
    stages = ((0, multiply), (0, add_core), (1, add_y), (2, add_z), (3, put))
    for turn in range(len(spans) + 3):
        for late, stage_of in stages:
            if 0 <= turn - late < len(spans):
                stage_of(turn - late)
    for c in started:
        c.wait_send()

    @pl.when(y == SIDE - 1)
    def _():
        prev_copy(1).wait_send()


def per_device(queries, latents, out_grad, layer_input, block_list):
    n_dp = lax.axis_size("dp")
    n_z = n_dp // 2
    n_heads = queries.shape[2]
    cols = layer_input.shape[2] // 16
    vmem = pl.BlockSpec(memory_space=pltpu.VMEM)
    hbm = pl.BlockSpec(memory_space=pl.ANY)
    dma = pltpu.SemaphoreType.DMA
    v = pltpu.VMEM
    widths = [(count + 127) // 128 * 128 for _, count in SPANS]
    n = len(SPANS)
    part = cols // 2
    lat_t, weight_grad = pl.pallas_call(
        kernel,
        out_shape=[jax.ShapeDtypeStruct((W, TOK), F32), jax.ShapeDtypeStruct((cols, W), F32)],
        in_specs=[pl.BlockSpec(memory_space=pltpu.SMEM), hbm, hbm, hbm, hbm],
        out_specs=[vmem, vmem],
        scratch_shapes=[
            v((n_heads, W, TOK), BF16),
            v((2, TOK, HEADS, R), BF16),
            v((n_heads, TOK, R), BF16),
            v((2, SIDE, HALF, TOK), BF16),
            v((2, 3, 2, HALF, TOK), BF16),
            v((2, SIDE, 2, HALF, TOK), BF16),
            v((2, HALF, TOK), BF16),
            v((SLOTS * TOK, W), BF16),
            v((n_heads // SUB, 2 * TOK, SUB * TOK), F32),
            v((n_heads // SUB, 2 * TOK, SUB * TOK), F32),
            v((SLOTS * TOK, W), F32),
            v((3, W, TOK), BF16),
            v((2, 3, 2, HALF, TOK), BF16),
            v((2, 3, HALF, TOK), BF16),
            v((2, 3, HALF, TOK), BF16),
            v((W, TOK), BF16),
            v((SIDE, W, TOK), BF16),
            v((SIDE, TOK, SIDE * cols), BF16),
            v((SIDE * cols, SIDE * TOK), BF16),
            [v((SIDE, part, w), BF16) for w in widths],
            [v((SIDE, part, w), BF16) for w in widths],
            [v((SIDE, part, w), BF16) for w in widths],
            [v((3, part, w), BF16) for w in widths],
            [v((n_z, part, w), BF16) for w in widths],
            [v((2, part, w), F32) for w in widths],
            dma((n_heads // HEADS,)), dma((2,)), dma((2,)), dma((2, 3)), dma((2, 3)), dma((2, 3)), dma((2, 3)), dma((2,)), dma((2,)),
            dma((3,)), dma((3,)), dma, dma((2, 3)), dma((2, 3)), dma((2, 3)), dma((2, 3)), dma((2,)), dma((2,)),
            dma((n, 3)), dma((n, 3)), dma((n,)), dma((n,)), dma((n, 3)), dma((n, 3)),
            dma((n, n_z - 1)), dma((n, n_z - 1)), dma((n,)), dma((n,)),
        ],
        compiler_params=pltpu.CompilerParams(
            collective_id=0, has_side_effects=True, vmem_limit_bytes=60 * 2**20
        ),
        name="attention_backward",
    )(
        block_list[0].T,
        latents.transpose(0, 2, 1),
        queries[0].transpose(1, 2, 0),
        out_grad[0],
        layer_input[0],
    )
    return (lat_t.T[None], weight_grad)


def solution(mesh):
    placed = (
        P("dp", "ctx", None, None),
        P("dp", "ctx", None),
        P("dp", "ctx", None, None),
        P("dp", "ctx", None),
        P("dp", None, None),
    )
    return jax.shard_map(
        per_device,
        mesh=mesh,
        in_specs=placed,
        out_specs=(P("dp", "ctx", None), P("ctx", None)),
        check_vma=False,
    )
```

time: 101 us -> 96.3 us (0.953)
  Pallas kernels: 94.4 us -> 91.7 us
  local copies, waits for them, and re-layouts: 5.14 us -> 3.78 us
    pallas_call x1, Pallas kernels: 94.4 us -> 91.7 us  [per_device(): pl.pallas_call(kernel, out_shape=[jax.ShapeDtypeStruct((W, TOK), F32), ja...]
    squeeze x1 -> x0, local copies, waits for them, and re-layouts: 1.36 us -> none  [per_device(): block_list[0]]
where the time goes in v3:
time: 96.3 us; the launch traced here: 96.1 us
  Pallas kernels  91.7 us (95%)
  local copies, waits for them, and re-layouts  3.78 us (4%)
    pallas_call x1, Pallas kernels, per_device(): pl.pallas_call(kernel, out_shape=[jax.ShapeDtypeStruct((W, TOK), F32), ja...  91.7 us
    unnamed x2, local copies, waits for them, and re-layouts  3.78 us

profile of v3, /device:TPU:1, one launch (start us, length us, event | category | flops | bytes accessed | tf_op | source)
XLA Modules:
  0.0 96.1 jit_solution(18008947369182309337)
XLA Ops:
  0.6 91.7 %attention_backward.1 = (f32[576,128]{1,0:T(8,128)}, f32[320,576]{1,0:T(8,128)}) custom-call(s32[4,16]{1,0:T(4,128)} %bitcast.17, bf16[1,576,128]{2,1,0:T(8,128)(2,1)} %bitcast.16, bf16[64,576,128]{2,1,0:T(8,128)(2,1)} %bitcast.12, bf16[128,64,512]{2,1,0:T(8,128)(2,1)} %bitcast.13, bf16[128,5120]{1,0:T(8,128)(2,1)} %bitcast.14), custom_call_target="tpu_custom_call" | custom-call | tf_op jit(solution)/shard_map/attention_backward/pallas_call | solution.py:445
  92.4 1.7 %copy.9 = f32[1,128,576]{1,2,0:T(8,128)} copy(f32[1,128,576]{1,2,0:T(8,128)} %bitcast.15) | data formatting | bytes 589824
  94.0 2.1 %copy.10 = f32[320,576]{1,0:T(8,128)} copy(f32[320,576]{1,0:T(8,128)} %get-tuple-element.9) | data formatting | bytes 1474560

commit v4 on v3

--- a/solution.py
+++ b/solution.py
@@ -86,9 +86,6 @@
         load.start()
     do_load(0).start()
     q_load(0).start()
-    do_load(1).start()
-    for i in range(1, steps):
-        q_load(i).start()
     x_own = pltpu.make_async_copy(
         inp.at[:, pl.ds(pl.multiple_of(x * quarter, 128), quarter)], xa.at[0], xo_s
     )
@@ -114,30 +111,20 @@
     def prev_copy(half):
         return remote(mine[half], prev.at[half], prev_s.at[half], prev_r.at[half], after)
 
-    start(prev_copy(0))
-
-    @pl.when(y == SIDE - 1)
-    def _():
-        prev_copy(1).start()
-
     for d in (1, 3, 2):
         for half in (0, 1):
             start(line_copy(half, d))
+    start(prev_copy(0))
+
+    @pl.when(y == SIDE - 1)
+    def _():
+        prev_copy(1).start()
+
+    do_load(1).start()
+    q_load(1).start()
     x_own.start()
 
     k_v[:TOK] = jnp.concatenate([line[0, x], line[1, y]], axis=0).T
-    prev_copy(0).wait_recv()
-    line_wait(1, 1)
-
-    @pl.when(y == 0)
-    def _():
-        prev_copy(1).wait_recv()
-        k_v[TOK : 2 * TOK] = jnp.concatenate([prev[0], prev[1]], axis=0).T
-
-    @pl.when(y > 0)
-    def _():
-        k_v[TOK : 2 * TOK] = jnp.concatenate([prev[0], line[1, (y + SIDE - 1) % SIDE]], axis=0).T
-
     def listed(device, e):
         block = jnp.maximum(lst[2 + e, device], 0)
         return block >> 2, block & 3
@@ -150,8 +137,7 @@
     def pass_on():
         for half in (0, 1):
             for d in (1, 2, 3):
-                if half == 0 or d > 1:
-                    line_wait(half, d)
+                line_wait(half, d)
         for d in (1, 3, 2, 0):
             for half in (0, 1):
                 for e in (0, 1):
@@ -176,19 +162,42 @@
         )
 
     per = HEADS // SUB
-    for i in range(steps):
+
+    def arrange(i):
         do_load(i).wait()
         q_load(i).wait()
         d_v[i * HEADS : (i + 1) * HEADS] = jnp.swapaxes(stage[i % 2], 0, 1)
         if i + 2 < steps:
             do_load(i + 2).start()
-
-        window = k_v[: 2 * TOK]
+            q_load(i + 2).start()
+
+    def window_products(i, rows):
+        keys = k_v[rows]
         for k in range(per):
             at = i * per + k
-            s_v[at], dp_v[at] = products(window, *columns(at))
+            s_v[at, rows], dp_v[at, rows] = products(keys, *columns(at))
+
+    for i in range(steps // 2):
+        arrange(i)
+        window_products(i, pl.ds(0, TOK))
         if i == 0:
             pass_on()
+    prev_copy(0).wait_recv()
+
+    @pl.when(y == 0)
+    def _():
+        prev_copy(1).wait_recv()
+        k_v[TOK : 2 * TOK] = jnp.concatenate([prev[0], prev[1]], axis=0).T
+
+    @pl.when(y > 0)
+    def _():
+        k_v[TOK : 2 * TOK] = jnp.concatenate([prev[0], line[1, (y + SIDE - 1) % SIDE]], axis=0).T
+
+    for i in range(steps // 2, steps):
+        arrange(i)
+        window_products(i, pl.ds(0, 2 * TOK))
+    for i in range(steps // 2):
+        window_products(i, pl.ds(TOK, TOK))
     for half in (0, 1):
         for d in (1, 2, 3):
             sel_copy(half, d).wait_recv()
@@ -284,15 +293,17 @@
         for half in (0, 1):
             start(raw_copy(half, d))
 
-    def near_copy(ch):
-        rows = pl.ds(*chunks[ch])
-        return remote(parts.at[0, rows], near.at[rows], near_s.at[ch], near_r.at[ch], before)
-
-    for ch in (0, 1):
-        first, count = chunks[ch]
+    def near_copy(half):
+        return remote(parts.at[0, halves[half]], near.at[half], near_s.at[half], near_r.at[half], before)
+
+    for first, count in chunks:
         window_grads(first, count)
-        parts[0, first : first + count] = acc[TOK : 2 * TOK, first : first + count].T.astype(BF16)
-        start(near_copy(ch))
+    parts[0] = acc[TOK : 2 * TOK].T.astype(BF16)
+    start(near_copy(0))
+
+    @pl.when(y == 0)
+    def _():
+        near_copy(1).start()
 
     x_own.wait()
     for d in range(SIDE):
@@ -322,18 +333,26 @@
             for entry, part in found:
                 term = part * jnp.where(entry == target, 1.0, 0.0)
                 added = term if added is None else added + term
+            if half == 1 and d == 3:
+                added += parts[0, halves[1]].astype(F32) * jnp.where(y > 0, 1.0, 0.0)
             if d == 0:
                 lat_ref[halves[half]] += added
             else:
                 mid[half, d - 1] = added.astype(BF16)
                 start(mid_copy(half, d))
 
-    for ch in (0, 1):
-        near_copy(ch).wait_recv()
+    near_copy(0).wait_recv()
     has_next = jnp.where(me < 15, 1.0, 0.0)
+
+    @pl.when(y == SIDE - 1)
+    def _():
+        near_copy(1).wait_recv()
+        lat_ref[LOW] += near[1].astype(F32) * has_next
+
+    lat_ref[TOP] += near[0].astype(F32) * has_next
     for half in (0, 1):
         rows = halves[half]
-        result = lat_ref[rows] + near[rows].astype(F32) * has_next
+        result = lat_ref[rows]
         for d in (1, 2, 3):
             mid_copy(half, d).wait_recv()
             result += back[half, d - 1].astype(F32)
@@ -417,8 +436,8 @@
     for ch in range(len(spans)):
         for d in (1, 3, 2):
             start(g_copy(ch, d))
-    stages = ((0, multiply), (0, add_core), (1, add_y), (2, add_z), (3, put))
-    for turn in range(len(spans) + 3):
+    stages = ((0, multiply), (1, add_core), (2, add_y), (3, add_z), (4, put))
+    for turn in range(len(spans) + 4):
         for late, stage_of in stages:
             if 0 <= turn - late < len(spans):
                 stage_of(turn - late)
@@ -428,6 +447,10 @@
     @pl.when(y == SIDE - 1)
     def _():
         prev_copy(1).wait_send()
+
+    @pl.when(y == 0)
+    def _():
+        near_copy(1).wait_send()
 
 
 def per_device(queries, latents, out_grad, layer_input, block_list):
@@ -463,7 +486,7 @@
             v((2, 3, 2, HALF, TOK), BF16),
             v((2, 3, HALF, TOK), BF16),
             v((2, 3, HALF, TOK), BF16),
-            v((W, TOK), BF16),
+            v((2, HALF, TOK), BF16),
             v((SIDE, W, TOK), BF16),
             v((SIDE, TOK, SIDE * cols), BF16),
             v((SIDE * cols, SIDE * TOK), BF16),

time: 96.3 us -> 90.6 us (0.941)
  Pallas kernels: 91.7 us -> 86 us
    pallas_call x1, Pallas kernels: 91.7 us -> 86 us  [per_device(): pl.pallas_call(kernel, out_shape=[jax.ShapeDtypeStruct((W, TOK), F32), ja...]
where the time goes in v4:
time: 90.6 us; the launch traced here: 90.4 us
  Pallas kernels  86 us (95%)
  local copies, waits for them, and re-layouts  3.78 us (4%)
    pallas_call x1, Pallas kernels, per_device(): pl.pallas_call(kernel, out_shape=[jax.ShapeDtypeStruct((W, TOK), F32), ja...  86 us
    unnamed x2, local copies, waits for them, and re-layouts  3.78 us

profile of v4, /device:TPU:1, one launch (start us, length us, event | category | flops | bytes accessed | tf_op | source)
XLA Modules:
  0.0 90.4 jit_solution(13232351317649504618)
XLA Ops:
  0.6 86.0 %attention_backward.1 = (f32[576,128]{1,0:T(8,128)}, f32[320,576]{1,0:T(8,128)}) custom-call(s32[4,16]{1,0:T(4,128)} %bitcast.17, bf16[1,576,128]{2,1,0:T(8,128)(2,1)} %bitcast.16, bf16[64,576,128]{2,1,0:T(8,128)(2,1)} %bitcast.12, bf16[128,64,512]{2,1,0:T(8,128)(2,1)} %bitcast.13, bf16[128,5120]{1,0:T(8,128)(2,1)} %bitcast.14), custom_call_target="tpu_custom_call" | custom-call | tf_op jit(solution)/shard_map/attention_backward/pallas_call | solution.py:468
  86.6 1.7 %copy.9 = f32[1,128,576]{1,2,0:T(8,128)} copy(f32[1,128,576]{1,2,0:T(8,128)} %bitcast.15) | data formatting | bytes 589824
  88.3 2.1 %copy.10 = f32[320,576]{1,0:T(8,128)} copy(f32[320,576]{1,0:T(8,128)} %get-tuple-element.9) | data formatting | bytes 1474560

commit v5 on v4

--- a/solution.py
+++ b/solution.py
@@ -13,7 +13,7 @@
 SIDE = 4
 HEADS = 16
 SUB = 4
-SPANS = ((0, 128), (128, 192), (320, 128), (448, 128))
+SPANS = ((0, 256), (256, 192), (448, 128))
 SCALE = 192 ** -0.5
 LOG2E = 1.4426950408889634
 NT = (((1,), (1,)), ((), ()))
@@ -390,9 +390,6 @@
         for d in (1, 2, 3):
             g_copy(ch, d).wait_recv()
         gt = jnp.concatenate([gbuf[d, pl.ds(*spans[ch])] for d in range(SIDE)], axis=1)
-        spare = cs[ch].shape[2] - gt.shape[0]
-        if spare:
-            gt = jnp.concatenate([gt, jnp.zeros((spare, gt.shape[1]), BF16)], axis=0)
         weight = lax.dot_general(xt[...], gt, NT, preferred_element_type=F32)
         for i in range(2 * SIDE):
             slot(ch, i // 2, i % 2)[...] = weight[i * part : (i + 1) * part]
@@ -431,13 +428,13 @@
         f_copy(ch, 1 - core).wait_recv()
         first, count = spans[ch]
         for i in (0, 1):
-            w_ref[i * part : (i + 1) * part, first : first + count] = fin[ch][i, :, :count]
+            w_ref[i * part : (i + 1) * part, first : first + count] = fin[ch][i]
 
     for ch in range(len(spans)):
         for d in (1, 3, 2):
             start(g_copy(ch, d))
-    stages = ((0, multiply), (1, add_core), (2, add_y), (3, add_z), (4, put))
-    for turn in range(len(spans) + 4):
+    stages = ((0, multiply), (0, add_core), (1, add_y), (2, add_z), (3, put))
+    for turn in range(len(spans) + 3):
         for late, stage_of in stages:
             if 0 <= turn - late < len(spans):
                 stage_of(turn - late)
@@ -451,6 +448,29 @@
     @pl.when(y == 0)
     def _():
         near_copy(1).wait_send()
+
+
+def deliver_kernel(lat_in, w_in, lat_out, w_out, sems):
+    copies = [
+        pltpu.make_async_copy(lat_in, lat_out, sems.at[0]),
+        pltpu.make_async_copy(w_in, w_out, sems.at[1]),
+    ]
+    for c in copies:
+        c.start()
+    for c in copies:
+        c.wait()
+
+
+def deliver(lat_t, weight_grad):
+    anywhere = pl.BlockSpec(memory_space=pl.ANY)
+    return pl.pallas_call(
+        deliver_kernel,
+        out_shape=[jax.ShapeDtypeStruct(a.shape, a.dtype) for a in (lat_t, weight_grad)],
+        in_specs=[anywhere, anywhere],
+        out_specs=[anywhere, anywhere],
+        scratch_shapes=[pltpu.SemaphoreType.DMA((2,))],
+        name="deliver",
+    )(lat_t, weight_grad)
 
 
 def per_device(queries, latents, out_grad, layer_input, block_list):
@@ -462,7 +482,7 @@
     hbm = pl.BlockSpec(memory_space=pl.ANY)
     dma = pltpu.SemaphoreType.DMA
     v = pltpu.VMEM
-    widths = [(count + 127) // 128 * 128 for _, count in SPANS]
+    widths = [count for _, count in SPANS]
     n = len(SPANS)
     part = cols // 2
     lat_t, weight_grad = pl.pallas_call(
@@ -512,6 +532,7 @@
         out_grad[0],
         layer_input[0],
     )
+    lat_t, weight_grad = deliver(lat_t, weight_grad)
     return (lat_t.T[None], weight_grad)
 
 

time: 90.6 us -> 120 us (1.32)
  Pallas kernels: 86 us -> 119 us
  local copies, waits for them, and re-layouts: 3.78 us -> 0 us
    pallas_call x0 -> x1, Pallas kernels: none -> 34.9 us  [deliver(): pl.pallas_call(deliver_kernel, out_shape=[jax.ShapeDtypeStruct(a.shape, a...]
    unnamed x2 -> x0, local copies, waits for them, and re-layouts: 3.78 us -> none
    pallas_call x1, Pallas kernels: 86 us -> 84.5 us  [per_device(): pl.pallas_call(kernel, out_shape=[jax.ShapeDtypeStruct((W, TOK), F32), ja...]
where the time goes in v5:
time: 120 us
  Pallas kernels  119 us (99%)
    pallas_call x1, Pallas kernels, per_device(): pl.pallas_call(kernel, out_shape=[jax.ShapeDtypeStruct((W, TOK), F32), ja...  84.5 us
    pallas_call x1, Pallas kernels, deliver(): pl.pallas_call(deliver_kernel, out_shape=[jax.ShapeDtypeStruct(a.shape, a...  34.9 us

profile of v5, /device:TPU:1, one launch (start us, length us, event | category | flops | bytes accessed | tf_op | source)
XLA Modules:
  0.0 120.1 jit_solution(5821139201897693489)
XLA Ops:
  0.6 84.5 %attention_backward.1 = (f32[576,128]{1,0:T(8,128)}, f32[320,576]{1,0:T(8,128)}) custom-call(s32[4,16]{1,0:T(4,128)} %bitcast.16, bf16[1,576,128]{2,1,0:T(8,128)(2,1)} %bitcast.15, bf16[64,576,128]{2,1,0:T(8,128)(2,1)} %bitcast.12, bf16[128,64,512]{2,1,0:T(8,128)(2,1)} %bitcast.13, bf16[128,5120]{1,0:T(8,128)(2,1)} %bitcast.14), custom_call_target="tpu_custom_call" | custom-call | tf_op jit(solution)/shard_map/attention_backward/pallas_call | solution.py:488
  85.1 34.9 %deliver.1 = (f32[576,128]{1,0:T(8,128)}, f32[320,576]{1,0:T(8,128)}) custom-call(f32[576,128]{1,0:T(8,128)} %get-tuple-element.6.lat_in, f32[320,576]{1,0:T(8,128)} %get-tuple-element.7.w_in), custom_call_target="tpu_custom_call" | custom-call | tf_op jit(solution)/shard_map/deliver/pallas_call | solution.py:466

commit v6 on v5

--- a/solution.py
+++ b/solution.py
@@ -450,25 +450,18 @@
         near_copy(1).wait_send()
 
 
-def deliver_kernel(lat_in, w_in, lat_out, w_out, sems):
-    copies = [
-        pltpu.make_async_copy(lat_in, lat_out, sems.at[0]),
-        pltpu.make_async_copy(w_in, w_out, sems.at[1]),
-    ]
-    for c in copies:
-        c.start()
-    for c in copies:
-        c.wait()
+def deliver_kernel(lat_in, w_in, lat_out, w_out):
+    lat_out[...] = lat_in[...]
+    w_out[...] = w_in[...]
 
 
 def deliver(lat_t, weight_grad):
-    anywhere = pl.BlockSpec(memory_space=pl.ANY)
+    vmem = pl.BlockSpec(memory_space=pltpu.VMEM)
     return pl.pallas_call(
         deliver_kernel,
         out_shape=[jax.ShapeDtypeStruct(a.shape, a.dtype) for a in (lat_t, weight_grad)],
-        in_specs=[anywhere, anywhere],
-        out_specs=[anywhere, anywhere],
-        scratch_shapes=[pltpu.SemaphoreType.DMA((2,))],
+        in_specs=[vmem, vmem],
+        out_specs=[vmem, vmem],
         name="deliver",
     )(lat_t, weight_grad)
 

time: 120 us -> 87.5 us (0.73)
  Pallas kernels: 119 us -> 86.7 us
    pallas_call x1, Pallas kernels: 34.9 us -> 2.25 us  [deliver(): pl.pallas_call(deliver_kernel, out_shape=[jax.ShapeDtypeStruct(a.shape, a...]
where the time goes in v6:
time: 87.5 us; the launch traced here: 87.3 us
  Pallas kernels  86.7 us (99%)
    pallas_call x1, Pallas kernels, per_device(): pl.pallas_call(kernel, out_shape=[jax.ShapeDtypeStruct((W, TOK), F32), ja...  84.5 us
    pallas_call x1, Pallas kernels, deliver(): pl.pallas_call(deliver_kernel, out_shape=[jax.ShapeDtypeStruct(a.shape, a...  2.25 us

profile of v6, /device:TPU:1, one launch (start us, length us, event | category | flops | bytes accessed | tf_op | source)
XLA Modules:
  0.0 87.3 jit_solution(13808582583198491938)
XLA Ops:
  0.6 84.5 %attention_backward.1 = (f32[576,128]{1,0:T(8,128)}, f32[320,576]{1,0:T(8,128)}) custom-call(s32[4,16]{1,0:T(4,128)} %bitcast.16, bf16[1,576,128]{2,1,0:T(8,128)(2,1)} %bitcast.15, bf16[64,576,128]{2,1,0:T(8,128)(2,1)} %bitcast.12, bf16[128,64,512]{2,1,0:T(8,128)(2,1)} %bitcast.13, bf16[128,5120]{1,0:T(8,128)(2,1)} %bitcast.14), custom_call_target="tpu_custom_call" | custom-call | tf_op jit(solution)/shard_map/attention_backward/pallas_call | solution.py:481
  85.1 2.2 %deliver.1 = (f32[576,128]{1,0:T(8,128)}, f32[320,576]{1,0:T(8,128)}) custom-call(f32[576,128]{1,0:T(8,128)} %get-tuple-element.6.lat_in, f32[320,576]{1,0:T(8,128)} %get-tuple-element.7.w_in), custom_call_target="tpu_custom_call" | custom-call | tf_op jit(solution)/shard_map/deliver/pallas_call | solution.py:460
